TPU v7x, 32 devices: a whole 2x2x4 slice. The times are simulated.
32 devices in a mesh: section: 4 (over y, x), tp: 4 (over z), seq: 2 (over core).
Axes of the slice: x: 2, y: 2, z: 4, core: 2. Of those that a mesh axis runs over, the one named last changes fastest.
Arguments:
- residual_entering: float32 [4, 2, 512, 1024], P(None, 'seq', None, 'tp'), may hold values from -6 to 6
- upstream_sensitivity: float32 [4, 2, 512, 1024], P(None, 'seq', None, 'tp'), may hold values from -6 to 6
- piece_lead_lines: float32 [4, 4, 2, 1024], P(None, None, 'seq', 'tp'), may hold values from -6 to 6
- dividend_start: float32 [2, 4, 2, 1024], P(None, None, 'seq', 'tp'), may hold values from -6 to 6
- divisor_start: float32 [2, 4, 2, 1024], P(None, None, 'seq', 'tp'), may hold values from 0.5 to 4
- power_offset_start: float32 [2, 4, 2, 1024], P(None, None, 'seq', 'tp'), may hold values from -2 to 2
- attend_standard_scale: float32 [2, 1024], P(None, 'tp'), may hold values from 0.5 to 1.5
- attend_standard_offset: float32 [2, 1024], P(None, 'tp'), may hold values from -1.5 to 1.5
- attend_lag_fractions: float32 [2, 3, 1024], P(None, None, 'tp'), may hold values from 0.05 to 0.95
- fading_log_rate: float32 [2, 1024], P(None, 'tp'), may hold values from -6 to -1
- reward_first_word: float32 [2, 1024], P(None, 'tp'), may hold values from -1 to 1
- attend_entry_matrix: bfloat16 [2, 3, 1024, 1024], P(None, None, None, 'tp'), may hold values from -0.1875 to 0.1875
- attend_exit_matrix: bfloat16 [2, 1024, 1024], P(None, 'tp'), may hold values from -0.75 to 0.75
- feed_standard_scale: float32 [2, 1024], P(None, 'tp'), may hold values from 0.5 to 1.5
- feed_standard_offset: float32 [2, 1024], P(None, 'tp'), may hold values from -1.5 to 1.5
- feed_lag_fractions: float32 [2, 2, 1024], P(None, None, 'tp'), may hold values from 0.05 to 0.95
- feed_lookup_matrix: bfloat16 [2, 1024, 4096], P(None, None, 'tp'), may hold values from -0.1875 to 0.1875
- feed_content_matrix: bfloat16 [2, 4096, 1024], P(None, 'tp'), may hold values from -0.09375 to 0.09375
- feed_gate_matrix: bfloat16 [2, 1024, 1024], P(None, None, 'tp'), may hold values from -0.1875 to 0.1875
Outputs:
- outputs: float32 [4, 2, 512, 1024], P(None, 'seq', 'section', 'tp')
- inputs_grad: float32 [4, 2, 512, 1024], P(None, 'seq', 'section', 'tp')
- prev_grad: float32 [4, 4, 2, 1024], P(None, None, 'seq', 'tp')
- num_grad: float32 [2, 4, 2, 1024], P(None, None, 'seq', 'tp')
- den_grad: float32 [2, 4, 2, 1024], P(None, None, 'seq', 'tp')
- max_grad: float32 [2, 4, 2, 1024], P(None, None, 'seq', 'tp')
- tm_gain_grad: float32 [2, 1024], P(None, 'tp')
- tm_bias_grad: float32 [2, 1024], P(None, 'tp')
- tm_mix_grad: float32 [2, 3, 1024], P(None, None, 'tp')
- decay_grad: float32 [2, 1024], P(None, 'tp')
- bonus_grad: float32 [2, 1024], P(None, 'tp')
- tm_in_grad: float32 [2, 3, 1024, 1024], P(None, None, None, 'tp')
- tm_out_grad: float32 [2, 1024, 1024], P(None, 'tp')
- cm_gain_grad: float32 [2, 1024], P(None, 'tp')
- cm_bias_grad: float32 [2, 1024], P(None, 'tp')
- cm_mix_grad: float32 [2, 2, 1024], P(None, None, 'tp')
- cm_key_grad: float32 [2, 1024, 4096], P(None, None, 'tp')
- cm_value_grad: float32 [2, 4096, 1024], P(None, 'tp')
- cm_recept_grad: float32 [2, 1024, 1024], P(None, None, 'tp')
All inputs are finite; a program needn't handle non-finite values.
Results may differ from a plain program's by a relative error of at most 0.013.
Values may be sent and summed in bfloat16 or wider, within the bound.
A program may use at most 448 MiB of HBM per device.

v0:
```python
from functools import partial

import jax
import jax.numpy as jnp
from jax import lax
from jax.sharding import PartitionSpec as P

BLOCK = 128


epsilon = 1e-05


def shifted_2(value, axis, steps):
    count = lax.axis_size(axis)
    first, last = (max(0, -steps), min(count, count - steps))
    return lax.ppermute(value, axis, [(source, source + steps) for source in range(first, last)])


def product(left_side, right_side):
    return jnp.dot(left_side, right_side, preferred_element_type=jnp.float32)


def inner_rows(left_side, right_side):
    return lax.dot_general(
        left_side, right_side, (((0,), (0,)), ((), ())), preferred_element_type=jnp.float32
    )


def against(left_side, right_side):
    return lax.dot_general(
        left_side, right_side, (((1,), (1,)), ((), ())), preferred_element_type=jnp.float32
    )


def keep_slot(store_in, micro_slot, is_valid, new_value):
    return store_in.at[micro_slot].set(jnp.where(is_valid, new_value, store_in[micro_slot]))


def weighted_value_blocks(
    block_length,
    incoming_lookups,
    incoming_contents,
    fading_entries,
    reward_entries,
    dividend_entries,
    divisor_entries,
    peak_line,
):
    decay_rate = jnp.exp(fading_entries)
    total_rows, channels = incoming_lookups.shape
    places = jnp.arange(block_length, dtype=jnp.float32)
    earlier = places[:, None] > places[None, :]
    spacing = places[:, None] - 1.0 - places[None, :]
    remain = block_length - 1.0 - places

    def advance(state_in, block_in):
        numer_in, denom_in, topmost = state_in
        lookup_piece_tile, value_block = block_in
        spread_exp = lookup_piece_tile[None, :, :] - spacing[:, :, None] * decay_rate
        spread_exp = jnp.where(earlier[:, :, None], spread_exp, -1e30)
        leading_power = reward_entries + lookup_piece_tile
        start_exp = topmost[None, :] - places[:, None] * decay_rate
        peak_exp = jnp.maximum(jnp.maximum(jnp.max(spread_exp, axis=1), leading_power), start_exp)
        weights = jnp.exp(spread_exp - peak_exp[:, None, :])
        from_state = jnp.exp(start_exp - peak_exp)
        own_term = jnp.exp(leading_power - peak_exp)
        numer_out = (
            from_state * numer_in
            + jnp.sum(weights * value_block[None, :, :], axis=1)
            + own_term * value_block
        )
        denom_out = from_state * denom_in + jnp.sum(weights, axis=1) + own_term
        ending = lookup_piece_tile - remain[:, None] * decay_rate
        stopping = topmost - block_length * decay_rate
        new_top = jnp.maximum(jnp.max(ending, axis=0), stopping)
        scaled = jnp.exp(ending - new_top[None, :])
        carried = jnp.exp(stopping - new_top)
        new_numer = carried * numer_in + jnp.sum(scaled * value_block, axis=0)
        new_denom = carried * denom_in + jnp.sum(scaled, axis=0)
        return ((new_numer, new_denom, new_top), numer_out / denom_out)

    blocks = total_rows // block_length
    unused, results = lax.scan(
        jax.checkpoint(advance),
        (dividend_entries, divisor_entries, peak_line),
        (
            incoming_lookups.reshape(blocks, block_length, channels),
            incoming_contents.reshape(blocks, block_length, channels),
        ),
    )
    return results.reshape(total_rows, channels)


def per_device(
    residual_entering,
    upstream_sensitivity,
    piece_lead_lines,
    dividend_start,
    divisor_start,
    power_offset_start,
    attend_standard_scale,
    attend_standard_offset,
    attend_lag_fractions,
    fading_log_rate,
    reward_first_word,
    attend_entry_matrix,
    attend_exit_matrix,
    feed_standard_scale,
    feed_standard_offset,
    feed_lag_fractions,
    feed_lookup_matrix,
    feed_content_matrix,
    feed_gate_matrix,
):
    sections = lax.axis_size("section")
    my_section = lax.axis_index("section")
    picked_level = my_section // 2
    is_channel = my_section % 2 == 1
    channel_weight = is_channel.astype(jnp.float32)
    time_weight = 1.0 - channel_weight
    micro_count = residual_entering.shape[0]
    length = residual_entering.shape[2]
    share_width = residual_entering.shape[3]
    features = share_width * lax.axis_size("tp")
    scale_entries = jnp.where(
        is_channel, feed_standard_scale[picked_level], attend_standard_scale[picked_level]
    )
    offset_entries = jnp.where(
        is_channel, feed_standard_offset[picked_level], attend_standard_offset[picked_level]
    )
    padded_mix = jnp.concatenate(
        [feed_lag_fractions[picked_level], jnp.zeros((1, share_width), jnp.float32)], axis=0
    )
    mix_share = jnp.where(is_channel, padded_mix, attend_lag_fractions[picked_level])

    def spread(incoming_lines, micro_slot, second_pass):
        first_sum = jnp.sum(incoming_lines, axis=1)
        second_sum = jnp.sum(incoming_lines * incoming_lines, axis=1)
        if second_pass:
            total_first, total_second = lax.psum((first_sum, second_sum), "tp")
        else:
            total_first, total_second = lax.psum((first_sum, second_sum), "tp")
        mean_row = total_first / features
        inv_std = lax.rsqrt(total_second / features - mean_row * mean_row + epsilon)
        normal_share = (incoming_lines - mean_row[:, None]) * inv_std[:, None]
        normed_share = normal_share * scale_entries + offset_entries
        small_share = jnp.concatenate(
            [piece_lead_lines[my_section, micro_slot, 0][None, :], mix_share], axis=0
        )
        if second_pass:
            normed_full, small_full = (
                lax.all_gather(normed_share, "tp", axis=1, tiled=True),
                lax.all_gather(small_share, "tp", axis=1, tiled=True),
            )
        else:
            normed_full, small_full = (
                lax.all_gather(normed_share, "tp", axis=1, tiled=True),
                lax.all_gather(small_share, "tp", axis=1, tiled=True),
            )
        return (normed_full, small_full, normal_share, inv_std)

    def mixtures(normed_full, small_full, mix_count):
        shifted = jnp.concatenate([small_full[0:1], normed_full[:-1]], axis=0)
        mixed_rows = [
            (
                normed_full * small_full[position + 1] + shifted * (1.0 - small_full[position + 1])
            ).astype(jnp.bfloat16)
            for position in range(mix_count)
        ]
        return (mixed_rows, shifted)

    def mix_back(normed_full, shifted, small_full, mix_grads):
        to_normed = jnp.zeros_like(normed_full)
        to_shifted = jnp.zeros_like(normed_full)
        ratio_grads = []
        for position, mix_grad in enumerate(mix_grads):
            mix_ratio = small_full[position + 1]
            to_normed = to_normed + mix_grad * mix_ratio
            to_shifted = to_shifted + mix_grad * (1.0 - mix_ratio)
            ratio_grads.append(jnp.sum(mix_grad * (normed_full - shifted), axis=0))
        for position in range(3 - len(mix_grads)):
            ratio_grads.append(jnp.zeros((normed_full.shape[1],), jnp.float32))
        to_normed = to_normed + jnp.concatenate(
            [to_shifted[1:], jnp.zeros_like(to_shifted[:1])], axis=0
        )
        small_grad = jnp.stack([to_shifted[0]] + ratio_grads)
        return (to_normed, small_grad)

    def wkv_inputs(lookups_here, contents_here, micro_slot):
        return (
            lookups_here,
            contents_here,
            fading_log_rate[picked_level],
            reward_first_word[picked_level],
            dividend_start[picked_level, micro_slot, 0],
            divisor_start[picked_level, micro_slot, 0],
            power_offset_start[picked_level, micro_slot, 0],
        )

    def time_zero():
        blank = jnp.zeros((share_width,), jnp.float32)
        return (
            jnp.zeros(attend_entry_matrix.shape[1:], jnp.float32),
            jnp.zeros(attend_exit_matrix.shape[1:], jnp.float32),
            blank,
            blank,
            blank,
            blank,
            blank,
        )

    def time_forward(normed_full, small_full, micro_slot):
        mixed_rows, shifted = mixtures(normed_full, small_full, 3)
        entry_matrix = attend_entry_matrix[picked_level]
        lookups_here = product(mixed_rows[0], entry_matrix[0])
        contents_here = product(mixed_rows[1], entry_matrix[1])
        recept = product(mixed_rows[2], entry_matrix[2])
        averaged_content_lines = weighted_value_blocks(
            BLOCK, *wkv_inputs(lookups_here, contents_here, micro_slot)
        )
        output = (jax.nn.sigmoid(recept) * averaged_content_lines).astype(jnp.bfloat16)
        return (product(output, attend_exit_matrix[picked_level]), jnp.ones_like(recept))

    def channel_forward(normed_full, small_full, micro_slot):
        mixed_rows, shifted = mixtures(normed_full, small_full, 2)
        hidden_pre = product(mixed_rows[0], feed_lookup_matrix[picked_level])
        hidden = jnp.square(jax.nn.softplus(hidden_pre)).astype(jnp.bfloat16)
        gate_pre = product(mixed_rows[1], feed_gate_matrix[picked_level])
        return (product(hidden, feed_content_matrix[picked_level]), jax.nn.sigmoid(gate_pre))

    def time_backward(normed_full, small_full, branch_grad, rows_grad, kv_share, micro_slot):
        mixed_rows, shifted = mixtures(normed_full, small_full, 3)
        entry_matrix = attend_entry_matrix[picked_level]
        exit_matrix = attend_exit_matrix[picked_level]
        lookups_here = product(mixed_rows[0], entry_matrix[0])
        contents_here = product(mixed_rows[1], entry_matrix[1])
        recept = product(mixed_rows[2], entry_matrix[2])
        averaged_content_lines, pullback = jax.vjp(
            partial(weighted_value_blocks, BLOCK),
            *wkv_inputs(lookups_here, contents_here, micro_slot)
        )
        gate_open = jax.nn.sigmoid(recept)
        output = (gate_open * averaged_content_lines).astype(jnp.bfloat16)
        out_grad = inner_rows(output, branch_grad)
        output_grad = against(branch_grad, exit_matrix)
        state_grads = pullback(output_grad * gate_open)
        pre_grads = [
            state_grads[0].astype(jnp.bfloat16),
            state_grads[1].astype(jnp.bfloat16),
            (output_grad * averaged_content_lines * gate_open * (1.0 - gate_open)).astype(
                jnp.bfloat16
            ),
        ]
        in_grad = jnp.stack(
            [inner_rows(mixed_rows[position], pre_grads[position]) for position in range(3)]
        )
        mix_grads = [against(pre_grads[position], entry_matrix[position]) for position in range(3)]
        to_normed, small_grad = mix_back(normed_full, shifted, small_full, mix_grads)
        attend_fraction = (
            in_grad,
            out_grad,
            state_grads[2],
            state_grads[3],
            state_grads[4],
            state_grads[5],
            state_grads[6],
        )
        return (
            to_normed,
            small_grad,
            attend_fraction,
            (
                jnp.zeros(feed_lookup_matrix.shape[1:], jnp.float32),
                jnp.zeros(feed_content_matrix.shape[1:], jnp.float32),
                jnp.zeros(feed_gate_matrix.shape[1:], jnp.float32),
            ),
        )

    def channel_backward(normed_full, small_full, branch_grad, rows_grad, kv_share, micro_slot):
        mixed_rows, shifted = mixtures(normed_full, small_full, 2)
        w_key = feed_lookup_matrix[picked_level]
        w_value = feed_content_matrix[picked_level]
        w_recept = feed_gate_matrix[picked_level]
        hidden_pre = product(mixed_rows[0], w_key)
        soft_part = jax.nn.softplus(hidden_pre)
        hidden = jnp.square(soft_part).astype(jnp.bfloat16)
        gate_open = jax.nn.sigmoid(product(mixed_rows[1], w_recept))
        value_grad = inner_rows(hidden, branch_grad)
        hidden_grad = (
            against(branch_grad, w_value) * 2.0 * soft_part * jax.nn.sigmoid(hidden_pre)
        ).astype(jnp.bfloat16)
        gate_grad = (rows_grad * kv_share * gate_open * (1.0 - gate_open)).astype(jnp.bfloat16)
        key_grad = inner_rows(mixed_rows[0], hidden_grad)
        recept_grad = inner_rows(mixed_rows[1], gate_grad)
        mix_grads = [against(hidden_grad, w_key), against(gate_grad, w_recept)]
        to_normed, small_grad = mix_back(normed_full, shifted, small_full, mix_grads)
        return (to_normed, small_grad, time_zero(), (key_grad, value_grad, recept_grad))

    carried = jnp.zeros((length, share_width), jnp.float32)
    saved_in = jnp.zeros((micro_count, length, share_width), jnp.float32)
    saved_kv = jnp.zeros_like(saved_in)
    saved_gate = jnp.zeros_like(saved_in)
    saved_out = jnp.zeros_like(saved_in)
    for moment in range(micro_count + sections - 1):
        micro_index = moment - my_section
        is_valid = (micro_index >= 0) & (micro_index < micro_count)
        micro_slot = jnp.clip(micro_index, 0, micro_count - 1)
        incoming_lines = jnp.where(my_section == 0, residual_entering[micro_slot, 0], carried)
        normed_full, small_full, normal_share, inv_std = spread(incoming_lines, micro_slot, False)
        branch_rows, gate_share = lax.cond(
            is_channel, channel_forward, time_forward, normed_full, small_full, micro_slot
        )
        kv_share = lax.psum_scatter(branch_rows, "tp", scatter_dimension=1, tiled=True)
        rows_out = incoming_lines + gate_share * kv_share
        saved_in = keep_slot(saved_in, micro_slot, is_valid, incoming_lines)
        saved_kv = keep_slot(saved_kv, micro_slot, is_valid, kv_share)
        saved_gate = keep_slot(saved_gate, micro_slot, is_valid, gate_share)
        saved_out = keep_slot(saved_out, micro_slot, is_valid, rows_out)
        carried = shifted_2(rows_out, "section", 1)
    grad_tm_gain = jnp.zeros(attend_standard_scale.shape, jnp.float32)
    grad_tm_bias = jnp.zeros(attend_standard_offset.shape, jnp.float32)
    grad_tm_mix = jnp.zeros(attend_lag_fractions.shape, jnp.float32)
    grad_decay = jnp.zeros(fading_log_rate.shape, jnp.float32)
    reward_derivative = jnp.zeros(reward_first_word.shape, jnp.float32)
    grad_tm_in = jnp.zeros(attend_entry_matrix.shape, jnp.float32)
    grad_tm_out = jnp.zeros(attend_exit_matrix.shape, jnp.float32)
    grad_cm_gain = jnp.zeros(feed_standard_scale.shape, jnp.float32)
    grad_cm_bias = jnp.zeros(feed_standard_offset.shape, jnp.float32)
    grad_cm_mix = jnp.zeros(feed_lag_fractions.shape, jnp.float32)
    grad_cm_key = jnp.zeros(feed_lookup_matrix.shape, jnp.float32)
    grad_cm_value = jnp.zeros(feed_content_matrix.shape, jnp.float32)
    grad_cm_recept = jnp.zeros(feed_gate_matrix.shape, jnp.float32)
    grad_prev = jnp.zeros(piece_lead_lines.shape, jnp.float32)
    grad_num = jnp.zeros(dividend_start.shape, jnp.float32)
    grad_den = jnp.zeros(divisor_start.shape, jnp.float32)
    grad_top = jnp.zeros(power_offset_start.shape, jnp.float32)
    returned = jnp.zeros((length, share_width), jnp.float32)
    saved_back = jnp.zeros_like(saved_in)
    for moment in range(micro_count + sections - 1):
        micro_index = moment - (sections - 1 - my_section)
        is_valid = (micro_index >= 0) & (micro_index < micro_count)
        micro_slot = jnp.clip(micro_index, 0, micro_count - 1)
        rows_grad = jnp.where(
            my_section == sections - 1, upstream_sensitivity[micro_slot, 0], returned
        )
        normed_full, small_full, normal_share, inv_std = spread(
            saved_in[micro_slot], micro_slot, True
        )
        gate_share = saved_gate[micro_slot]
        branch_grad = lax.all_gather(
            (rows_grad * gate_share).astype(jnp.bfloat16), "tp", axis=1, tiled=True
        )
        normed_part, small_part, attend_fraction, channel_part = lax.cond(
            is_channel,
            channel_backward,
            time_backward,
            normed_full,
            small_full,
            branch_grad,
            rows_grad,
            saved_kv[micro_slot],
            micro_slot,
        )
        normed_grad, small_grad = (
            lax.psum_scatter(normed_part, "tp", scatter_dimension=1, tiled=True),
            lax.psum_scatter(small_part, "tp", scatter_dimension=1, tiled=True),
        )
        scaled_grad = normed_grad * scale_entries
        first_sum = jnp.sum(scaled_grad, axis=1)
        second_sum = jnp.sum(scaled_grad * normal_share, axis=1)
        total_first, total_second = lax.psum((first_sum, second_sum), "tp")
        rows_back = rows_grad + inv_std[:, None] * (
            scaled_grad
            - total_first[:, None] / features
            - normal_share * (total_second[:, None] / features)
        )
        valid_weight = is_valid.astype(jnp.float32)
        attend_factor = valid_weight * time_weight
        channel_scale = valid_weight * channel_weight
        gain_grad = jnp.sum(normed_grad * normal_share, axis=0)
        bias_grad = jnp.sum(normed_grad, axis=0)
        grad_tm_gain = grad_tm_gain.at[picked_level].add(attend_factor * gain_grad)
        grad_tm_bias = grad_tm_bias.at[picked_level].add(attend_factor * bias_grad)
        grad_cm_gain = grad_cm_gain.at[picked_level].add(channel_scale * gain_grad)
        grad_cm_bias = grad_cm_bias.at[picked_level].add(channel_scale * bias_grad)
        grad_tm_mix = grad_tm_mix.at[picked_level].add(attend_factor * small_grad[1:4])
        grad_cm_mix = grad_cm_mix.at[picked_level].add(channel_scale * small_grad[1:3])
        grad_prev = grad_prev.at[my_section, micro_slot, 0].add(valid_weight * small_grad[0])
        grad_tm_in = grad_tm_in.at[picked_level].add(attend_factor * attend_fraction[0])
        grad_tm_out = grad_tm_out.at[picked_level].add(attend_factor * attend_fraction[1])
        grad_decay = grad_decay.at[picked_level].add(attend_factor * attend_fraction[2])
        reward_derivative = reward_derivative.at[picked_level].add(
            attend_factor * attend_fraction[3]
        )
        grad_num = grad_num.at[picked_level, micro_slot, 0].add(attend_factor * attend_fraction[4])
        grad_den = grad_den.at[picked_level, micro_slot, 0].add(attend_factor * attend_fraction[5])
        grad_top = grad_top.at[picked_level, micro_slot, 0].add(attend_factor * attend_fraction[6])
        grad_cm_key = grad_cm_key.at[picked_level].add(channel_scale * channel_part[0])
        grad_cm_value = grad_cm_value.at[picked_level].add(channel_scale * channel_part[1])
        grad_cm_recept = grad_cm_recept.at[picked_level].add(channel_scale * channel_part[2])
        saved_back = keep_slot(saved_back, micro_slot, is_valid, rows_back)
        returned = shifted_2(rows_back, "section", -1)
    out_part = jnp.where(my_section == sections - 1, saved_out, 0.0)[:, None]
    back_part = jnp.where(my_section == 0, saved_back, 0.0)[:, None]
    out_share, back_share = (
        lax.psum_scatter(out_part, "section", scatter_dimension=2, tiled=True),
        lax.psum_scatter(back_part, "section", scatter_dimension=2, tiled=True),
    )
    totals = lax.psum(
        (
            grad_tm_gain,
            grad_tm_bias,
            grad_tm_mix,
            grad_decay,
            reward_derivative,
            grad_tm_in,
            grad_tm_out,
            grad_cm_gain,
            grad_cm_bias,
            grad_cm_mix,
            grad_cm_key,
            grad_cm_value,
            grad_cm_recept,
        ),
        ("section", "seq"),
    )
    state_totals = lax.psum((grad_prev, grad_num, grad_den, grad_top), "section")
    return (
        out_share,
        back_share,
        state_totals[0],
        state_totals[1],
        state_totals[2],
        state_totals[3],
        totals[0],
        totals[1],
        totals[2],
        totals[3],
        totals[4],
        totals[5],
        totals[6],
        totals[7],
        totals[8],
        totals[9],
        totals[10],
        totals[11],
        totals[12],
    )


def solution(mesh):
    placed = (
        P(None, "seq", None, "tp"),
        P(None, "seq", None, "tp"),
        P(None, None, "seq", "tp"),
        P(None, None, "seq", "tp"),
        P(None, None, "seq", "tp"),
        P(None, None, "seq", "tp"),
        P(None, "tp"),
        P(None, "tp"),
        P(None, None, "tp"),
        P(None, "tp"),
        P(None, "tp"),
        P(None, None, None, "tp"),
        P(None, "tp", None),
        P(None, "tp"),
        P(None, "tp"),
        P(None, None, "tp"),
        P(None, None, "tp"),
        P(None, "tp", None),
        P(None, None, "tp"),
    )
    return jax.shard_map(
        per_device,
        mesh=mesh,
        in_specs=placed,
        out_specs=(
            P(None, "seq", "section", "tp"),
            P(None, "seq", "section", "tp"),
            P(None, None, "seq", "tp"),
            P(None, None, "seq", "tp"),
            P(None, None, "seq", "tp"),
            P(None, None, "seq", "tp"),
            P(None, "tp"),
            P(None, "tp"),
            P(None, None, "tp"),
            P(None, "tp"),
            P(None, "tp"),
            P(None, None, None, "tp"),
            P(None, "tp", None),
            P(None, "tp"),
            P(None, "tp"),
            P(None, None, "tp"),
            P(None, None, "tp"),
            P(None, "tp", None),
            P(None, None, "tp"),
        ),
        check_vma=False,
    )
```

profile of v0, /device:TPU:9, one launch (start us, length us, event | category | flops | bytes accessed | tf_op | source)
XLA Modules:
  0.0 5374.8 jit_solution(7396340874890131246)
XLA Ops:
  67.7 90.7 %conditional.14 = (f32[512,1024]{1,0:T(8,128)}, f32[512,256]{1,0:T(8,128)}) conditional(s32[]{:T(128)} %convert_element_type.677, (f32[4,1024]{1,0:T(4,128)S(1)}, f32[512,1024]{1,0:T(8,128)}, s32[]{:T(128)}, bf16[2,3,1024,256]{3,2,1,0:T(8,128)(2,1)}, s32[]{:T(128)}, /*index=5*/f32[2,4,1,256]{3,2,1,0:T(1,128)S(1)}, f32[2,4,1,256]{3,2,1,0:T(1,128)S(1)}, ...), branch_computations={%region_5.14_spmd, %region_14.15_spmd} | conditional | flops 2425751552 | bytes 34967932 | solution.py:311
  73.5 78.9 %while.644 = (s32[]{:T(128)}, f32[256]{0:T(256)S(1)}, f32[256]{0:T(256)S(1)}, f32[256]{0:T(256)S(1)}, f32[4,128,256]{2,1,0:T(8,128)}, /*index=5*/f32[256]{0:T(25...) while((s32[]{:T(128)}, f32[256]{0:T(256)S(1)}, ...), condition=%wide.region_13.13_spmd.clone.clone.clone, body=%wide.region_6.12_spmd.clone.clone.sunk.clone | while | flops 47024000 | bytes 2900089 | solution.py:84
  159.7 40.0 reduce-scatter.38.cloned.1.call-done
  241.3 39.5 all-gather.24.cloned.1.call-done
  280.8 90.6 %conditional.15 = (f32[512,1024]{1,0:T(8,128)}, f32[512,256]{1,0:T(8,128)}) conditional(s32[]{:T(128)} %convert_element_type.677, (f32[4,1024]{1,0:T(4,128)S(1)}, f32[512,1024]{1,0:T(8,128)}, s32[]{:T(128)}, bf16[2,3,1024,256]{3,2,1,0:T(8,128)(2,1)S(1)}, s32[]{:T(128)}, /*index=5*/f32[2,4,1,256]{3,2,1,0:T(1,128)S(1)}, ...), branch_computations={%region_21.30_spmd, %region_30.31_spmd} | conditional | flops 2425751552 | bytes 22384992 | solution.py:311
  286.5 78.9 %while.645 = (s32[]{:T(128)}, f32[256]{0:T(256)S(1)}, f32[256]{0:T(256)S(1)}, f32[256]{0:T(256)S(1)}, f32[4,128,256]{2,1,0:T(8,128)}, /*index=5*/f32[256]{0:T(25...) while((s32[]{:T(128)}, f32[256]{0:T(256)S(1)}, ...), condition=%wide.region_29.29_spmd.clone.clone.clone, body=%wide.region_22.28_spmd.clone.clone.sunk.clone | while | flops 47024000 | bytes 2900089 | solution.py:84
  454.1 39.3 all-gather.26.cloned.1.call-done
  493.4 90.8 %conditional.16 = (f32[512,1024]{1,0:T(8,128)}, f32[512,256]{1,0:T(8,128)}) conditional(s32[]{:T(128)} %convert_element_type.677, (f32[4,1024]{1,0:T(4,128)S(1)}, f32[512,1024]{1,0:T(8,128)}, s32[]{:T(128)}, bf16[2,3,1024,256]{3,2,1,0:T(8,128)(2,1)S(1)}, s32[]{:T(128)}, /*index=5*/f32[2,4,1,256]{3,2,1,0:T(1,128)S(1)}, ...), branch_computations={%region_37.46_spmd, %region_46.47_spmd} | conditional | flops 2425751552 | bytes 22384992 | solution.py:311
  499.3 78.9 %while.646 = (s32[]{:T(128)}, f32[256]{0:T(256)S(1)}, f32[256]{0:T(256)S(1)}, f32[256]{0:T(256)S(1)}, f32[4,128,256]{2,1,0:T(8,128)}, /*index=5*/f32[256]{0:T(25...) while((s32[]{:T(128)}, f32[256]{0:T(256)S(1)}, ...), condition=%wide.region_45.45_spmd.clone.clone.clone, body=%wide.region_38.44_spmd.clone.clone.sunk.clone | while | flops 47024000 | bytes 2900089 | solution.py:84
  667.0 39.1 all-gather.28.cloned.1.call-done
  706.1 90.6 %conditional.17 = (f32[512,1024]{1,0:T(8,128)}, f32[512,256]{1,0:T(8,128)}) conditional(s32[]{:T(128)} %convert_element_type.677, (f32[4,1024]{1,0:T(4,128)S(1)}, f32[512,1024]{1,0:T(8,128)}, s32[]{:T(128)}, bf16[2,3,1024,256]{3,2,1,0:T(8,128)(2,1)S(1)}, s32[]{:T(128)}, /*index=5*/f32[2,4,1,256]{3,2,1,0:T(1,128)S(1)}, ...), branch_computations={%region_53.62_spmd, %region_62.63_spmd} | conditional | flops 2425751552 | bytes 22384992 | solution.py:311
  711.7 78.9 %while.647 = (s32[]{:T(128)}, f32[256]{0:T(256)S(1)}, f32[256]{0:T(256)S(1)}, f32[256]{0:T(256)S(1)}, f32[4,128,256]{2,1,0:T(8,128)}, /*index=5*/f32[256]{0:T(25...) while((s32[]{:T(128)}, f32[256]{0:T(256)S(1)}, ...), condition=%wide.region_61.61_spmd.clone.clone.clone, body=%wide.region_54.60_spmd.clone.clone.sunk.clone | while | flops 47024000 | bytes 2900089 | solution.py:84
  879.3 39.2 all-gather.30.cloned.1.call-done
  918.5 90.6 %conditional.18 = (f32[512,1024]{1,0:T(8,128)}, f32[512,256]{1,0:T(8,128)}) conditional(s32[]{:T(128)} %convert_element_type.677, (f32[4,1024]{1,0:T(4,128)S(1)}, f32[512,1024]{1,0:T(8,128)}, s32[]{:T(128)}, bf16[2,3,1024,256]{3,2,1,0:T(8,128)(2,1)S(1)}, s32[]{:T(128)}, /*index=5*/f32[2,4,1,256]{3,2,1,0:T(1,128)S(1)}, ...), branch_computations={%region_69.78_spmd, %region_78.79_spmd} | conditional | flops 2425751552 | bytes 22384992 | solution.py:311
  924.2 78.9 %while.648 = (s32[]{:T(128)}, f32[256]{0:T(256)S(1)}, f32[256]{0:T(256)S(1)}, f32[256]{0:T(256)S(1)}, f32[4,128,256]{2,1,0:T(8,128)}, /*index=5*/f32[256]{0:T(25...) while((s32[]{:T(128)}, f32[256]{0:T(256)S(1)}, ...), condition=%wide.region_77.77_spmd.clone.clone.clone, body=%wide.region_70.76_spmd.clone.clone.sunk.clone | while | flops 47024000 | bytes 2900089 | solution.py:84
  1091.8 39.2 all-gather.32.cloned.1.call-done
  1131.0 90.9 %conditional.19 = (f32[512,1024]{1,0:T(8,128)}, f32[512,256]{1,0:T(8,128)}) conditional(s32[]{:T(128)} %convert_element_type.677, (f32[4,1024]{1,0:T(4,128)S(1)}, f32[512,1024]{1,0:T(8,128)}, s32[]{:T(128)}, bf16[2,3,1024,256]{3,2,1,0:T(8,128)(2,1)S(1)}, s32[]{:T(128)}, /*index=5*/f32[2,4,1,256]{3,2,1,0:T(1,128)S(1)}, ...), branch_computations={%region_85.94_spmd, %region_94.95_spmd} | conditional | flops 2425751552 | bytes 22384992 | solution.py:311
  1136.9 78.9 %while.649 = (s32[]{:T(128)}, f32[256]{0:T(256)S(1)}, f32[256]{0:T(256)S(1)}, f32[256]{0:T(256)S(1)}, f32[4,128,256]{2,1,0:T(8,128)}, /*index=5*/f32[256]{0:T(25...) while((s32[]{:T(128)}, f32[256]{0:T(256)S(1)}, ...), condition=%wide.region_93.93_spmd.clone.clone.clone, body=%wide.region_86.92_spmd.clone.clone.sunk.clone | while | flops 47024000 | bytes 2900089 | solution.py:84
  1348.2 90.6 %conditional.20 = (f32[512,1024]{1,0:T(8,128)}, f32[512,256]{1,0:T(8,128)}) conditional(s32[]{:T(128)} %convert_element_type.677, (f32[4,1024]{1,0:T(4,128)S(1)}, f32[512,1024]{1,0:T(8,128)}, s32[]{:T(128)}, bf16[2,3,1024,256]{3,2,1,0:T(8,128)(2,1)S(1)}, s32[]{:T(128)}, /*index=5*/f32[2,4,1,256]{3,2,1,0:T(1,128)S(1)}, ...), branch_computations={%region_101.110_spmd, %region_110.111_spmd} | conditional | flops 2425751552 | bytes 22384992 | solution.py:311
  1353.8 78.9 %while.650 = (s32[]{:T(128)}, f32[256]{0:T(256)S(1)}, f32[256]{0:T(256)S(1)}, f32[256]{0:T(256)S(1)}, f32[4,128,256]{2,1,0:T(8,128)}, /*index=5*/f32[256]{0:T(25...) while((s32[]{:T(128)}, f32[256]{0:T(256)S(1)}, ...), condition=%wide.region_109.109_spmd.clone.clone.clone, body=%wide.region_102.108_spmd.clone.clone.sunk.clone | while | flops 47024000 | bytes 2900089 | solution.py:84
  1557.5 324.6 %conditional.21 = (f32[512,1024]{1,0:T(8,128)}, f32[4,1024]{1,0:T(4,128)S(1)}, f32[3,1024,256]{2,1,0:T(8,128)}, f32[256,1024]{1,0:T(8,128)}, f32[256]{0:T(256)S(...) conditional(s32[]{:T(128)} %convert_element_type.677, ...), branch_computations={%region_118.149_spmd, %region_149.152_spmd} | conditional | flops 6197620736 | bytes 134793888 | solution.py:354
  1568.6 93.3 %while.652 = (s32[]{:T(128)}, f32[256]{0:T(256)S(1)}, f32[256]{0:T(256)S(1)}, f32[256]{0:T(256)S(1)}, f32[4,128,256]{2,1,0:T(8,128)}, /*index=5*/f32[4,256]{1,0:...) while((s32[]{:T(128)}, f32[256]{0:T(256)S(1)}, ...), condition=%wide.region_126.126_spmd.clone.clone.clone, body=%wide.region_119.125_spmd.clone.clone.sunk.clone | while | flops 46990336 | bytes 2823349 | solution.py:84
  1673.5 190.9 %while.651 = (s32[]{:T(128)}, f32[256]{0:T(256)}, f32[256]{0:T(256)}, f32[256]{0:T(256)}, f32[256]{0:T(256)}, /*index=5*/f32[256]{0:T(256)}, bf16[4,128,256]{2,1...) while((s32[]{:T(128)}, f32[256]{0:T(256)}, ...), condition=%wide.region_145.145_spmd.clone.clone, body=%wide.region_127.144_spmd.clone.sunk.clone | while | flops 167683200 | bytes 14122826 | solution.py:84
  1985.6 48.5 all-gather.42.cloned.1.call-done
  2034.2 325.8 %conditional.22 = (f32[512,1024]{1,0:T(8,128)}, f32[4,1024]{1,0:T(4,128)S(1)}, f32[3,1024,256]{2,1,0:T(8,128)}, f32[256,1024]{1,0:T(8,128)}, f32[256]{0:T(256)S(...) conditional(s32[]{:T(128)} %convert_element_type.677, ...), branch_computations={%region_162.193_spmd, %region_193.196_spmd} | conditional | flops 6197620736 | bytes 134793888 | solution.py:354
  2046.4 93.3 %while.654 = (s32[]{:T(128)}, f32[256]{0:T(256)S(1)}, f32[256]{0:T(256)S(1)}, f32[256]{0:T(256)S(1)}, f32[4,128,256]{2,1,0:T(8,128)}, /*index=5*/f32[4,256]{1,0:...) while((s32[]{:T(128)}, f32[256]{0:T(256)S(1)}, ...), condition=%wide.region_170.170_spmd.clone.clone.clone, body=%wide.region_163.169_spmd.clone.clone.sunk.clone | while | flops 46990336 | bytes 2823349 | solution.py:84
  2151.4 191.1 %while.653 = (s32[]{:T(128)}, f32[256]{0:T(256)}, f32[256]{0:T(256)}, f32[256]{0:T(256)}, f32[256]{0:T(256)}, /*index=5*/f32[256]{0:T(256)}, bf16[4,128,256]{2,1...) while((s32[]{:T(128)}, f32[256]{0:T(256)}, ...), condition=%wide.region_189.189_spmd.clone.clone, body=%wide.region_171.188_spmd.clone.sunk.clone | while | flops 167683200 | bytes 14122826 | solution.py:84
  2460.6 48.7 all-gather.46.cloned.1.call-done
  2509.3 326.3 %conditional.23 = (f32[512,1024]{1,0:T(8,128)}, f32[4,1024]{1,0:T(4,128)S(1)}, f32[3,1024,256]{2,1,0:T(8,128)}, f32[256,1024]{1,0:T(8,128)}, f32[256]{0:T(256)S(...) conditional(s32[]{:T(128)} %convert_element_type.677, ...), branch_computations={%region_206.237_spmd, %region_237.240_spmd} | conditional | flops 6197620736 | bytes 134793888 | solution.py:354
  2521.8 93.3 %while.656 = (s32[]{:T(128)}, f32[256]{0:T(256)S(1)}, f32[256]{0:T(256)S(1)}, f32[256]{0:T(256)S(1)}, f32[4,128,256]{2,1,0:T(8,128)}, /*index=5*/f32[4,256]{1,0:...) while((s32[]{:T(128)}, f32[256]{0:T(256)S(1)}, ...), condition=%wide.region_214.214_spmd.clone.clone.clone, body=%wide.region_207.213_spmd.clone.clone.sunk.clone | while | flops 46990336 | bytes 2823349 | solution.py:84
  2626.8 191.2 %while.655 = (s32[]{:T(128)}, f32[256]{0:T(256)}, f32[256]{0:T(256)}, f32[256]{0:T(256)}, f32[256]{0:T(256)}, /*index=5*/f32[256]{0:T(256)}, bf16[4,128,256]{2,1...) while((s32[]{:T(128)}, f32[256]{0:T(256)}, ...), condition=%wide.region_233.233_spmd.clone.clone, body=%wide.region_215.232_spmd.clone.sunk.clone | while | flops 167683200 | bytes 14122826 | solution.py:84
  2936.4 48.4 all-gather.50.cloned.1.call-done
  2984.8 326.2 %conditional.24 = (f32[512,1024]{1,0:T(8,128)}, f32[4,1024]{1,0:T(4,128)S(1)}, f32[3,1024,256]{2,1,0:T(8,128)}, f32[256,1024]{1,0:T(8,128)}, f32[256]{0:T(256)S(...) conditional(s32[]{:T(128)} %convert_element_type.677, ...), branch_computations={%region_250.281_spmd, %region_281.284_spmd} | conditional | flops 6197620736 | bytes 134793888 | solution.py:354
  2997.3 93.3 %while.658 = (s32[]{:T(128)}, f32[256]{0:T(256)S(1)}, f32[256]{0:T(256)S(1)}, f32[256]{0:T(256)S(1)}, f32[4,128,256]{2,1,0:T(8,128)}, /*index=5*/f32[4,256]{1,0:...) while((s32[]{:T(128)}, f32[256]{0:T(256)S(1)}, ...), condition=%wide.region_258.258_spmd.clone.clone.clone, body=%wide.region_251.257_spmd.clone.clone.sunk.clone | while | flops 46990336 | bytes 2823349 | solution.py:84
  3102.3 190.9 %while.657 = (s32[]{:T(128)}, f32[256]{0:T(256)}, f32[256]{0:T(256)}, f32[256]{0:T(256)}, f32[256]{0:T(256)}, /*index=5*/f32[256]{0:T(256)}, bf16[4,128,256]{2,1...) while((s32[]{:T(128)}, f32[256]{0:T(256)}, ...), condition=%wide.region_277.277_spmd.clone.clone, body=%wide.region_259.276_spmd.clone.sunk.clone | while | flops 167683200 | bytes 14122826 | solution.py:84
  3411.4 48.7 all-gather.54.cloned.1.call-done
  3460.1 325.7 %conditional.25 = (f32[512,1024]{1,0:T(8,128)}, f32[4,1024]{1,0:T(4,128)S(1)}, f32[3,1024,256]{2,1,0:T(8,128)}, f32[256,1024]{1,0:T(8,128)}, f32[256]{0:T(256)S(...) conditional(s32[]{:T(128)} %convert_element_type.677, ...), branch_computations={%region_294.325_spmd, %region_325.328_spmd} | conditional | flops 6197620736 | bytes 134793888 | solution.py:354
  3472.5 93.2 %while.660 = (s32[]{:T(128)}, f32[256]{0:T(256)S(1)}, f32[256]{0:T(256)S(1)}, f32[256]{0:T(256)S(1)}, f32[4,128,256]{2,1,0:T(8,128)}, /*index=5*/f32[4,256]{1,0:...) while((s32[]{:T(128)}, f32[256]{0:T(256)S(1)}, ...), condition=%wide.region_302.302_spmd.clone.clone.clone, body=%wide.region_295.301_spmd.clone.clone.sunk.clone | while | flops 46990336 | bytes 2823349 | solution.py:84
  3577.4 190.9 %while.659 = (s32[]{:T(128)}, f32[256]{0:T(256)}, f32[256]{0:T(256)}, f32[256]{0:T(256)}, f32[256]{0:T(256)}, /*index=5*/f32[256]{0:T(256)}, bf16[4,128,256]{2,1...) while((s32[]{:T(128)}, f32[256]{0:T(256)}, ...), condition=%wide.region_321.321_spmd.clone.clone, body=%wide.region_303.320_spmd.clone.sunk.clone | while | flops 167683200 | bytes 14122826 | solution.py:84
  3886.3 48.6 all-gather.58.cloned.1.call-done
  3934.9 326.0 %conditional.26 = (f32[512,1024]{1,0:T(8,128)}, f32[4,1024]{1,0:T(4,128)S(1)}, f32[3,1024,256]{2,1,0:T(8,128)}, f32[256,1024]{1,0:T(8,128)}, f32[256]{0:T(256)S(...) conditional(s32[]{:T(128)} %convert_element_type.677, ...), branch_computations={%region_338.369_spmd, %region_369.372_spmd} | conditional | flops 6197620736 | bytes 134793888 | solution.py:354
  3947.2 93.3 %while.662 = (s32[]{:T(128)}, f32[256]{0:T(256)S(1)}, f32[256]{0:T(256)S(1)}, f32[256]{0:T(256)S(1)}, f32[4,128,256]{2,1,0:T(8,128)}, /*index=5*/f32[4,256]{1,0:...) while((s32[]{:T(128)}, f32[256]{0:T(256)S(1)}, ...), condition=%wide.region_346.346_spmd.clone.clone.clone, body=%wide.region_339.345_spmd.clone.clone.sunk.clone | while | flops 46990336 | bytes 2823349 | solution.py:84
  4052.3 191.0 %while.661 = (s32[]{:T(128)}, f32[256]{0:T(256)}, f32[256]{0:T(256)}, f32[256]{0:T(256)}, f32[256]{0:T(256)}, /*index=5*/f32[256]{0:T(256)}, bf16[4,128,256]{2,1...) while((s32[]{:T(128)}, f32[256]{0:T(256)}, ...), condition=%wide.region_365.365_spmd.clone.clone, body=%wide.region_347.364_spmd.clone.sunk.clone | while | flops 167683200 | bytes 14122826 | solution.py:84
  4362.1 48.3 all-gather.62.cloned.1.call-done
  4410.4 324.0 %conditional.27 = (f32[512,1024]{1,0:T(8,128)S(1)}, f32[4,1024]{1,0:T(4,128)S(1)}, f32[3,1024,256]{2,1,0:T(8,128)}, f32[256,1024]{1,0:T(8,128)}, f32[256]{0:T(25...) conditional(s32[]{:T(128)} %convert_element_type.677, ...), branch_computations={%region_382.413_spmd, %region_413.416_spmd} | conditional | flops 6197620736 | bytes 134781520 | solution.py:354
  4422.6 93.5 %while.664 = (s32[]{:T(128)}, f32[256]{0:T(256)S(1)}, f32[256]{0:T(256)S(1)}, f32[256]{0:T(256)S(1)}, f32[4,128,256]{2,1,0:T(8,128)}, /*index=5*/f32[4,256]{1,0:...) while((s32[]{:T(128)}, f32[256]{0:T(256)S(1)}, ...), condition=%wide.region_390.390_spmd.clone.clone.clone, body=%wide.region_383.389_spmd.clone.clone.sunk.clone | while | flops 46990336 | bytes 2823349 | solution.py:84
  4527.8 190.1 %while.663 = (s32[]{:T(128)}, f32[256]{0:T(256)}, f32[256]{0:T(256)}, f32[256]{0:T(256)}, f32[256]{0:T(256)}, /*index=5*/f32[256]{0:T(256)}, bf16[4,128,256]{2,1...) while((s32[]{:T(128)}, f32[256]{0:T(256)}, ...), condition=%wide.region_409.409_spmd.clone.clone, body=%wide.region_391.408_spmd.clone.sunk.clone | while | flops 167683200 | bytes 14114578 | solution.py:84
  5092.4 256.1 %all-reduce.34.cloned.1.call-done = (f32[2,3,1024,256]{3,2,1,0:T(8,128)}, f32[2,256,1024]{2,1,0:T(8,128)}, f32[2,1024,1024]{2,1,0:T(8,128)}, f32[2,1024,1024]{2,1,0:T(8,128)}, f32[2,1024,256]{2,1,0:T(8,128)}) async-done(((f32[2,3,1024,256]{3,2,1,0:T(8,128)}, f32[2,256,1024]{2,1,0:T(8,128)}, f32[2,1024,1024]{2,1,0:T(8,128)}, f32[2,1024,1024]{2,1,0:T(8,128)}, f32[2,1024,256]{2,1,0:T(8,128)}), ...) | async-done | bytes 27262992 | tf_op jit(solution)/shard_map/psum | solution.py:410
  (3222 shorter events, 4561.0 us)
Async XLA Ops:
  7.3 60.4 %all-gather.22.cloned.1.call-start = ((), (), s32[]{:S(2)}) async-start(), calls=%async_computation.23 | async-start | bytes 2621440 | tf_op jit(solution)/shard_map/all_gather | solution.py:158
  20.5 179.2 %reduce-scatter.38.cloned.1.call-start = ((), (), s32[]{:S(2)}) async-start(), calls=%async_computation.24 | async-start | bytes 2621440 | tf_op jit(solution)/shard_map/reduce_scatter | solution.py:314
  158.4 122.4 %all-gather.24.cloned.1.call-start = ((), (), s32[]{:S(2)}) async-start(), calls=%async_computation.25 | async-start | bytes 2621440 | tf_op jit(solution)/shard_map/all_gather | solution.py:158
  231.8 180.9 %reduce-scatter.40.cloned.1.call-start = ((), (), s32[]{:S(2)}) async-start(), calls=%async_computation.26 | async-start | bytes 2621440 | tf_op jit(solution)/shard_map/reduce_scatter | solution.py:314
  371.4 122.0 %all-gather.26.cloned.1.call-start = ((), (), s32[]{:S(2)}) async-start(), calls=%async_computation.27 | async-start | bytes 2621440 | tf_op jit(solution)/shard_map/all_gather | solution.py:158
  445.2 180.3 %reduce-scatter.42.cloned.1.call-start = ((), (), s32[]{:S(2)}) async-start(), calls=%async_computation.28 | async-start | bytes 2621440 | tf_op jit(solution)/shard_map/reduce_scatter | solution.py:314
  584.2 121.8 %all-gather.28.cloned.1.call-start = ((), (), s32[]{:S(2)}) async-start(), calls=%async_computation.29 | async-start | bytes 2621440 | tf_op jit(solution)/shard_map/all_gather | solution.py:158
  629.4 13.9 collective-permute-start.2
  658.0 179.9 %reduce-scatter.44.cloned.1.call-start = ((), (), s32[]{:S(2)}) async-start(), calls=%async_computation.30 | async-start | bytes 2621440 | tf_op jit(solution)/shard_map/reduce_scatter | solution.py:314
  796.7 121.8 %all-gather.30.cloned.1.call-start = ((), (), s32[]{:S(2)}) async-start(), calls=%async_computation.31 | async-start | bytes 2621440 | tf_op jit(solution)/shard_map/all_gather | solution.py:158
  870.4 180.0 %reduce-scatter.46.cloned.1.call-start = ((), (), s32[]{:S(2)}) async-start(), calls=%async_computation.32 | async-start | bytes 2621440 | tf_op jit(solution)/shard_map/reduce_scatter | solution.py:314
  1009.1 121.8 %all-gather.32.cloned.1.call-start = ((), (), s32[]{:S(2)}) async-start(), calls=%async_computation.33 | async-start | bytes 2621440 | tf_op jit(solution)/shard_map/all_gather | solution.py:158
  1054.3 13.9 collective-permute-start.4
  1082.9 180.2 %reduce-scatter.48.cloned.1.call-start = ((), (), s32[]{:S(2)}) async-start(), calls=%async_computation.34 | async-start | bytes 2621440 | tf_op jit(solution)/shard_map/reduce_scatter | solution.py:314
  1221.8 126.3 %all-gather.34.cloned.1.call-start = ((), (), s32[]{:S(2)}) async-start(), calls=%async_computation.35 | async-start | bytes 2621440 | tf_op jit(solution)/shard_map/all_gather | solution.py:158
  1267.0 13.9 collective-permute-start.5
  1300.2 179.9 %reduce-scatter.50.cloned.1.call-start = ((), (), s32[]{:S(2)}) async-start(), calls=%async_computation.36 | async-start | bytes 2621440 | tf_op jit(solution)/shard_map/reduce_scatter | solution.py:314
  1438.8 89.4 %all-gather.38.cloned.1.call-start = ((), (), s32[]{:S(2)}) async-start(), calls=%async_computation.39 | async-start | bytes 2621440 | tf_op jit(solution)/shard_map/all_gather | solution.py:153
  1439.4 118.1 %all-gather.36.cloned.1.call-start = ((), (), s32[]{:S(2)}) async-start(), calls=%async_computation.38 | async-start | bytes 1310720 | tf_op jit(solution)/shard_map/all_gather | solution.py:351
  1486.0 439.6 %reduce-scatter.54.cloned.1.call-start = ((), (), s32[]{:S(2)}) async-start(), calls=%async_computation.40 | async-start | bytes 2621440 | tf_op jit(solution)/shard_map/reduce_scatter | solution.py:366
  1882.1 103.5 %all-gather.40.cloned.1.call-start = ((), (), s32[]{:S(2)}) async-start(), calls=%async_computation.41 | async-start | bytes 1310720 | tf_op jit(solution)/shard_map/all_gather | solution.py:351
  1956.2 78.0 %all-gather.42.cloned.1.call-start = ((), (), s32[]{:S(2)}) async-start(), calls=%async_computation.42 | async-start | bytes 2621440 | tf_op jit(solution)/shard_map/all_gather | solution.py:153
  1958.3 443.1 %reduce-scatter.56.cloned.1.call-start = ((), (), s32[]{:S(2)}) async-start(), calls=%async_computation.43 | async-start | bytes 2621440 | tf_op jit(solution)/shard_map/reduce_scatter | solution.py:366
  2360.1 100.5 %all-gather.44.cloned.1.call-start = ((), (), s32[]{:S(2)}) async-start(), calls=%async_computation.44 | async-start | bytes 1310720 | tf_op jit(solution)/shard_map/all_gather | solution.py:351
  2431.1 78.2 %all-gather.46.cloned.1.call-start = ((), (), s32[]{:S(2)}) async-start(), calls=%async_computation.45 | async-start | bytes 2621440 | tf_op jit(solution)/shard_map/all_gather | solution.py:153
  2433.3 443.8 %reduce-scatter.58.cloned.1.call-start = ((), (), s32[]{:S(2)}) async-start(), calls=%async_computation.46 | async-start | bytes 2621440 | tf_op jit(solution)/shard_map/reduce_scatter | solution.py:366
  2835.7 100.6 %all-gather.48.cloned.1.call-start = ((), (), s32[]{:S(2)}) async-start(), calls=%async_computation.47 | async-start | bytes 1310720 | tf_op jit(solution)/shard_map/all_gather | solution.py:351
  2906.7 78.1 %all-gather.50.cloned.1.call-start = ((), (), s32[]{:S(2)}) async-start(), calls=%async_computation.48 | async-start | bytes 2621440 | tf_op jit(solution)/shard_map/all_gather | solution.py:153
  2908.8 443.5 %reduce-scatter.60.cloned.1.call-start = ((), (), s32[]{:S(2)}) async-start(), calls=%async_computation.49 | async-start | bytes 2621440 | tf_op jit(solution)/shard_map/reduce_scatter | solution.py:366
  3311.0 100.4 %all-gather.52.cloned.1.call-start = ((), (), s32[]{:S(2)}) async-start(), calls=%async_computation.50 | async-start | bytes 1310720 | tf_op jit(solution)/shard_map/all_gather | solution.py:351
  3381.9 78.2 %all-gather.54.cloned.1.call-start = ((), (), s32[]{:S(2)}) async-start(), calls=%async_computation.51 | async-start | bytes 2621440 | tf_op jit(solution)/shard_map/all_gather | solution.py:153
  3384.1 443.2 %reduce-scatter.62.cloned.1.call-start = ((), (), s32[]{:S(2)}) async-start(), calls=%async_computation.52 | async-start | bytes 2621440 | tf_op jit(solution)/shard_map/reduce_scatter | solution.py:366
  3785.9 100.4 %all-gather.56.cloned.1.call-start = ((), (), s32[]{:S(2)}) async-start(), calls=%async_computation.53 | async-start | bytes 1310720 | tf_op jit(solution)/shard_map/all_gather | solution.py:351
  3856.8 78.1 %all-gather.58.cloned.1.call-start = ((), (), s32[]{:S(2)}) async-start(), calls=%async_computation.54 | async-start | bytes 2621440 | tf_op jit(solution)/shard_map/all_gather | solution.py:153
  3858.9 443.3 %reduce-scatter.64.cloned.1.call-start = ((), (), s32[]{:S(2)}) async-start(), calls=%async_computation.55 | async-start | bytes 2621440 | tf_op jit(solution)/shard_map/reduce_scatter | solution.py:366
  4261.0 101.1 %all-gather.60.cloned.1.call-start = ((), (), s32[]{:S(2)}) async-start(), calls=%async_computation.56 | async-start | bytes 1310720 | tf_op jit(solution)/shard_map/all_gather | solution.py:351
  4332.0 78.4 %all-gather.62.cloned.1.call-start = ((), (), s32[]{:S(2)}) async-start(), calls=%async_computation.57 | async-start | bytes 2621440 | tf_op jit(solution)/shard_map/all_gather | solution.py:153
  4334.7 459.3 %reduce-scatter.70.cloned.1.call-start = ((), (), s32[]{:S(2)}) async-start(), calls=%async_computation.60 | async-start | bytes 655360
  4335.8 495.6 %reduce-scatter.72.cloned.1.call-start = ((), (), s32[]{:S(2)}) async-start(), calls=%async_computation.61 | async-start | bytes 655360
  4337.0 533.7 %reduce-scatter.74.cloned.1.call-start = ((), (), s32[]{:S(2)}) async-start(), calls=%async_computation.62 | async-start | bytes 655360
  4338.1 571.1 %reduce-scatter.76.cloned.1.call-start = ((), (), s32[]{:S(2)}) async-start(), calls=%async_computation.63 | async-start | bytes 655360
  4339.2 598.5 %reduce-scatter.66.cloned.1.call-start = ((), (), s32[]{:S(2)}) async-start(), calls=%async_computation.58 | async-start | bytes 2621440 | tf_op jit(solution)/shard_map/reduce_scatter | solution.py:366
  4735.8 281.8 %reduce-scatter.78.cloned.1.call-start = ((), (), s32[]{:S(2)}) async-start(), calls=%async_computation.64 | async-start | bytes 655360
  4748.8 281.7 %reduce-scatter.80.cloned.1.call-start = ((), (), s32[]{:S(2)}) async-start(), calls=%async_computation.65 | async-start | bytes 655360
  4750.6 292.8 %reduce-scatter.82.cloned.1.call-start = ((), (), s32[]{:S(2)}) async-start(), calls=%async_computation.66 | async-start | bytes 655360
  4752.5 340.0 %reduce-scatter.52.cloned.1.call-start = ((), (), s32[]{:S(2)}) async-start(), calls=%async_computation.37 | async-start | bytes 2621440 | tf_op jit(solution)/shard_map/reduce_scatter | solution.py:407
  4754.1 338.3 %reduce-scatter.68.cloned.1.call-start = ((), (), s32[]{:S(2)}) async-start(), calls=%async_computation.59 | async-start | bytes 2621440 | tf_op jit(solution)/shard_map/reduce_scatter | solution.py:408
  4954.6 394.0 %all-reduce.34.cloned.1.call-start = ((), (), s32[]{:S(2)}) async-start(), calls=%async_computation.67 | async-start | bytes 54525952 | tf_op jit(solution)/shard_map/psum | solution.py:410
  (417 other events, 9809.1 us)
Sparse Core Ops, SparseCore 0:
  20.6 47.0 all-gather.21
  158.5 41.1 reduce-scatter.37
  231.9 48.8 all-gather.23
  371.6 41.1 reduce-scatter.39
  445.4 48.0 all-gather.25
  584.4 41.0 reduce-scatter.41
  658.1 47.9 all-gather.27
  796.8 41.0 reduce-scatter.43
  870.5 47.9 all-gather.29
  1009.2 41.0 reduce-scatter.45
  1083.0 47.9 all-gather.31
  1222.0 41.0 reduce-scatter.47
  1300.3 47.7 all-gather.33
  1438.9 41.1 reduce-scatter.49
  1482.2 45.9 all-gather.37
  1530.3 27.1 all-gather.35
  1882.3 43.2 reduce-scatter.53
  1956.3 29.3 all-gather.39
  1987.8 46.3 all-gather.41
  2360.2 41.1 reduce-scatter.55
  2431.2 29.3 all-gather.43
  2462.8 46.4 all-gather.45
  2835.8 41.1 reduce-scatter.57
  2906.8 29.5 all-gather.47
  2938.5 46.2 all-gather.49
  3311.1 41.1 reduce-scatter.59
  3382.0 29.3 all-gather.51
  3413.6 46.3 all-gather.53
  3786.0 41.1 reduce-scatter.61
  3856.9 29.3 all-gather.55
  3888.4 46.3 all-gather.57
  4261.1 41.1 reduce-scatter.63
  4332.1 29.9 all-gather.59
  4364.3 46.0 all-gather.61
  4412.7 18.3 reduce-scatter.69
  4433.3 19.9 reduce-scatter.71
  4455.6 19.9 reduce-scatter.73
  4477.9 19.9 reduce-scatter.75
  4735.9 41.0 reduce-scatter.65
  4779.3 19.5 reduce-scatter.77
  4801.2 19.8 reduce-scatter.79
  4823.3 19.8 reduce-scatter.81
  4847.2 37.2 reduce-scatter.51
  4954.7 34.5 reduce-scatter.67
  5014.3 334.1 all-reduce.33
where the time goes:
time: 5400 us; the launch traced here: 5370 us
  other arithmetic  2830 us (52%)
  waiting for transfers between devices  1520 us (28%)
  local copies, waits for them, and re-layouts  433 us (8%)
  blocking collectives  297 us (6%)
  matrix products  157 us (3%)
  starting transfers between devices  108 us (2%)
    reduce_sum x84, other arithmetic, advance(): jnp.sum(weights * value_block[None, :, :], axis=1)  705 us
    reduce_max x84, other arithmetic, advance(): jnp.max(spread_exp, axis=1)  614 us
    all_gather x14, waiting for transfers between devices, spread(): lax.all_gather(normed_share, 'tp', axis=1, tiled=True)  592 us
    reduce_sum x28, other arithmetic, advance(): lookup_piece_tile[None, :, :] - spacing[:, :, None] * decay_rate  325 us
    reduce_sum x28, other arithmetic, advance(): weights = jnp.exp(spread_exp - peak_exp[:, None, :])  289 us
    psum x1, waiting for transfers between devices, per_device(): lax.psum((grad_tm_gain, grad_tm_bias, grad_tm_mix, grad_decay, reward_der...  256 us
    reduce_scatter x7, waiting for transfers between devices, per_device(): lax.psum_scatter(branch_rows, 'tp', scatter_dimension=1, tiled=True)  251 us
    reduce_scatter x7, waiting for transfers between devices, per_device(): lax.psum_scatter(normed_part, 'tp', scatter_dimension=1, tiled=True)  170 us
  transfers between devices with their start and end apart: 57, of which 47 were waited for; matrix products, arithmetic and copies ran while one was open for 13% of the time, Pallas kernels for 0%

commit v1 on v0

v1 whole, which is shorter than its diff:
```python
from functools import partial

import jax
import jax.numpy as jnp
from jax import lax
from jax.experimental import pallas as pl
from jax.experimental.pallas import tpu as pltpu
from jax.sharding import PartitionSpec as P

BLOCK = 128


epsilon = 1e-05


def product(left_side, right_side):
    return jnp.dot(left_side, right_side, preferred_element_type=jnp.float32)


def inner_rows(left_side, right_side):
    return lax.dot_general(
        left_side, right_side, (((0,), (0,)), ((), ())), preferred_element_type=jnp.float32
    )


def against(left_side, right_side):
    return lax.dot_general(
        left_side, right_side, (((1,), (1,)), ((), ())), preferred_element_type=jnp.float32
    )


def weighted_value_blocks(
    block_length,
    incoming_lookups,
    incoming_contents,
    fading_entries,
    reward_entries,
    dividend_entries,
    divisor_entries,
    peak_line,
):
    decay_rate = jnp.exp(fading_entries)
    total_rows, channels = incoming_lookups.shape
    places = jnp.arange(block_length, dtype=jnp.float32)
    earlier = places[:, None] > places[None, :]
    spacing = places[:, None] - 1.0 - places[None, :]
    remain = block_length - 1.0 - places

    def advance(state_in, block_in):
        numer_in, denom_in, topmost = state_in
        lookup_piece_tile, value_block = block_in
        spread_exp = lookup_piece_tile[None, :, :] - spacing[:, :, None] * decay_rate
        spread_exp = jnp.where(earlier[:, :, None], spread_exp, -1e30)
        leading_power = reward_entries + lookup_piece_tile
        start_exp = topmost[None, :] - places[:, None] * decay_rate
        peak_exp = jnp.maximum(jnp.maximum(jnp.max(spread_exp, axis=1), leading_power), start_exp)
        weights = jnp.exp(spread_exp - peak_exp[:, None, :])
        from_state = jnp.exp(start_exp - peak_exp)
        own_term = jnp.exp(leading_power - peak_exp)
        numer_out = (
            from_state * numer_in
            + jnp.sum(weights * value_block[None, :, :], axis=1)
            + own_term * value_block
        )
        denom_out = from_state * denom_in + jnp.sum(weights, axis=1) + own_term
        ending = lookup_piece_tile - remain[:, None] * decay_rate
        stopping = topmost - block_length * decay_rate
        new_top = jnp.maximum(jnp.max(ending, axis=0), stopping)
        scaled = jnp.exp(ending - new_top[None, :])
        carried = jnp.exp(stopping - new_top)
        new_numer = carried * numer_in + jnp.sum(scaled * value_block, axis=0)
        new_denom = carried * denom_in + jnp.sum(scaled, axis=0)
        return ((new_numer, new_denom, new_top), numer_out / denom_out)

    blocks = total_rows // block_length
    unused, results = lax.scan(
        jax.checkpoint(advance),
        (dividend_entries, divisor_entries, peak_line),
        (
            incoming_lookups.reshape(blocks, block_length, channels),
            incoming_contents.reshape(blocks, block_length, channels),
        ),
    )
    return results.reshape(total_rows, channels)


def spread_plain(rows_in):
    features = rows_in.shape[1] * lax.axis_size("tp")
    mean_row = lax.psum(jnp.sum(rows_in, axis=1), "tp") / features
    center = rows_in - mean_row[:, None]
    inv_std = lax.rsqrt(lax.psum(jnp.sum(center * center, axis=1), "tp") / features + epsilon)
    normal_share = center * inv_std[:, None]
    normal_full = lax.all_gather(normal_share.astype(jnp.bfloat16), "tp", axis=1, tiled=True)
    return normal_share, inv_std, normal_full


def mix_plain(normal_full, small_full, mix_count):
    normed = normal_full.astype(jnp.float32) * small_full[0] + small_full[1]
    shifted = jnp.concatenate([small_full[2:3], normed[:-1]], axis=0)
    gap = normed - shifted
    mixed = [(shifted + gap * small_full[3 + i]).astype(jnp.bfloat16) for i in range(mix_count)]
    return mixed, gap


def scatter_plain(branch):
    return lax.psum_scatter(
        branch.astype(jnp.bfloat16), "tp", scatter_dimension=1, tiled=True
    ).astype(jnp.float32)


def time_forward_plain(rows_in, small_full, small_own, wkv_rows, entry_matrix, exit_matrix):
    normal_share, inv_std, normal_full = spread_plain(rows_in)
    mixed, gap = mix_plain(normal_full, small_full, 3)
    lookups, contents, recept = [product(mixed[i], entry_matrix[i]) for i in range(3)]
    averaged, pullback = jax.vjp(
        partial(weighted_value_blocks, BLOCK), lookups, contents, *[wkv_rows[i] for i in range(5)]
    )
    gate = jax.nn.sigmoid(recept)
    output = (gate * averaged).astype(jnp.bfloat16)
    rows_out = rows_in + scatter_plain(product(output, exit_matrix))
    kept = (normal_share, inv_std, normal_full, mixed, gap, averaged, pullback, gate, output)
    return rows_out, kept


def channel_forward_plain(rows_in, small_full, small_own, w_key, w_value, w_gate):
    normal_share, inv_std, normal_full = spread_plain(rows_in)
    mixed, gap = mix_plain(normal_full, small_full, 2)
    hidden_pre = product(mixed[0], w_key)
    soft = jax.nn.softplus(hidden_pre)
    hidden = jnp.square(soft).astype(jnp.bfloat16)
    gate = jax.nn.sigmoid(product(mixed[1], w_gate))
    kv_share = scatter_plain(product(hidden, w_value))
    kept = (normal_share, inv_std, normal_full, mixed, gap, hidden_pre, soft, hidden, gate, kv_share)
    return rows_in + gate * kv_share, kept


def norm_back_plain(rows_grad, mix_grads, gap, normal_full, normal_share, inv_std, small_full, small_own):
    share = normal_share.shape[1]
    features = small_full.shape[1]
    to_normed = sum(grad * small_full[3 + i] for i, grad in enumerate(mix_grads))
    to_shifted = sum(grad * (1.0 - small_full[3 + i]) for i, grad in enumerate(mix_grads))
    ratio_grads = [jnp.sum(grad * gap, axis=0) for grad in mix_grads]
    ratio_grads += [jnp.zeros_like(ratio_grads[0])] * (3 - len(mix_grads))
    to_normed = to_normed + jnp.concatenate([to_shifted[1:], jnp.zeros_like(to_shifted[:1])], axis=0)
    normed_grad = scatter_plain(to_normed)
    edge = lax.psum_scatter(
        jnp.stack([to_shifted[0]] + ratio_grads), "tp", scatter_dimension=1, tiled=True
    )
    scaled = normed_grad * small_own[0]
    first, second = lax.psum((jnp.sum(scaled, axis=1), jnp.sum(scaled * normal_share, axis=1)), "tp")
    rows_back = rows_grad + inv_std[:, None] * (
        scaled - first[:, None] / features - normal_share * (second[:, None] / features)
    )
    gain_grad = jnp.sum(normed_grad * normal_share, axis=0)
    bias_grad = jnp.sum(normed_grad, axis=0)
    zero = jnp.zeros((2, share), jnp.float32)
    return rows_back, jnp.concatenate([gain_grad[None], bias_grad[None], edge, zero], axis=0)


def time_backward_plain(rows_grad, kept, small_full, small_own, wkv_rows, entry_matrix, exit_matrix):
    normal_share, inv_std, normal_full, mixed, gap, averaged, pullback, gate, output = kept
    branch_grad = lax.all_gather(rows_grad.astype(jnp.bfloat16), "tp", axis=1, tiled=True)
    exit_grad = inner_rows(output, branch_grad)
    output_grad = against(branch_grad, exit_matrix)
    state_grads = pullback(output_grad * gate)
    pre_grads = [
        state_grads[0].astype(jnp.bfloat16),
        state_grads[1].astype(jnp.bfloat16),
        (output_grad * averaged * gate * (1.0 - gate)).astype(jnp.bfloat16),
    ]
    entry_grad = jnp.stack([inner_rows(mixed[i], pre_grads[i]) for i in range(3)])
    mix_grads = [against(pre_grads[i], entry_matrix[i]) for i in range(3)]
    rows_back, small_grad = norm_back_plain(
        rows_grad, mix_grads, gap, normal_full, normal_share, inv_std, small_full, small_own
    )
    wkv_grad = jnp.concatenate([jnp.stack(state_grads[2:]), jnp.zeros((3, gate.shape[1]))], axis=0)
    return rows_back, small_grad, wkv_grad, (entry_grad.astype(jnp.bfloat16), exit_grad.astype(jnp.bfloat16))


def channel_backward_plain(rows_grad, kept, small_full, small_own, w_key, w_value, w_gate):
    normal_share, inv_std, normal_full, mixed, gap, hidden_pre, soft, hidden, gate, kv_share = kept
    branch_grad = lax.all_gather((rows_grad * gate).astype(jnp.bfloat16), "tp", axis=1, tiled=True)
    value_grad = inner_rows(hidden, branch_grad)
    hidden_grad = (
        against(branch_grad, w_value) * 2.0 * soft * jax.nn.sigmoid(hidden_pre)
    ).astype(jnp.bfloat16)
    gate_grad = (rows_grad * kv_share * gate * (1.0 - gate)).astype(jnp.bfloat16)
    key_grad = inner_rows(mixed[0], hidden_grad)
    recept_grad = inner_rows(mixed[1], gate_grad)
    mix_grads = [against(hidden_grad, w_key), against(gate_grad, w_gate)]
    rows_back, small_grad = norm_back_plain(
        rows_grad, mix_grads, gap, normal_full, normal_share, inv_std, small_full, small_own
    )
    grads = tuple(grad.astype(jnp.bfloat16) for grad in (key_grad, value_grad, recept_grad))
    return rows_back, small_grad, grads


CHUNK = 128
LANES = 128
SUB = 8
MESH = pl.DeviceIdType.MESH
NO_POWER = -1e30


def to_row_tile(*columns):
    lane = lax.broadcasted_iota(jnp.int32, (CHUNK, LANES), 1)
    wide = jnp.zeros((CHUNK, LANES), jnp.float32)
    for place, column in enumerate(columns):
        wide = jnp.where(lane == place, column, wide)
    return jnp.transpose(wide)[:SUB]


def to_columns(tiles):
    count = len(tiles)
    filler = [jnp.zeros((LANES - SUB * count, CHUNK), jnp.float32)]
    return jnp.transpose(jnp.concatenate(list(tiles) + filler, axis=0))


STEP = CHUNK // SUB


def shift_rows(value, first_row):
    ends = pltpu.roll(value[CHUNK - SUB :], 1, 0)
    at = lax.broadcasted_iota(jnp.int32, ends.shape, 0)
    return jnp.concatenate([jnp.where(at == 0, first_row, ends), value[: CHUNK - SUB]], axis=0)


def unshift_rows(value, last_row):
    starts = pltpu.roll(value[:SUB], SUB - 1, 0)
    at = lax.broadcasted_iota(jnp.int32, starts.shape, 0)
    return jnp.concatenate([value[SUB:], jnp.where(at == SUB - 1, last_row, starts)], axis=0)


def to_stretches(tokens_ref, rows_ref):
    def step(c, unused):
        base = pl.multiple_of(c * CHUNK, CHUNK)
        for s in range(STEP):
            for g in range(tokens_ref.shape[0]):
                rows_ref[pl.ds(base + s * SUB, SUB), g * LANES : (g + 1) * LANES] = tokens_ref[
                    g, pl.ds(base + s, SUB, stride=STEP), :
                ]
        return unused

    lax.fori_loop(0, rows_ref.shape[0] // CHUNK, step, 0)


def to_tokens(rows_ref, tokens_ref, c):
    base = pl.multiple_of(c * CHUNK, CHUNK)
    for s in range(STEP):
        for g in range(tokens_ref.shape[0]):
            tokens_ref[g, pl.ds(base + s, SUB, stride=STEP), :] = rows_ref[
                pl.ds(base + s * SUB, SUB), g * LANES : (g + 1) * LANES
            ]


class Peers:
    def __init__(self, count, width):
        self.count, self.width = count, width
        self.me = lax.axis_index("tp")

    def to(self, k):
        return lax.rem(self.me + k, self.count)

    def source(self, k):
        return lax.rem(self.me + self.count - k, self.count)

    def columns(self, owner):
        if isinstance(owner, int):
            return slice(owner * self.width, (owner + 1) * self.width)
        return pl.ds(pl.multiple_of(owner * self.width, LANES), self.width)

    def greet(self, others):
        barrier = pltpu.get_barrier_semaphore()
        places = [{"tp": self.to(k)} for k in range(1, self.count)] + others
        for place in places:
            pl.semaphore_signal(barrier, inc=1, device_id=place, device_id_type=MESH)
        pl.semaphore_wait(barrier, len(places))

    def copy(self, device, source_ref, target_ref, send, receive):
        return pltpu.make_async_remote_copy(
            src_ref=source_ref, dst_ref=target_ref, send_sem=send, recv_sem=receive,
            device_id={"tp": device}, device_id_type=MESH,
        )


def rows_of(c):
    return pl.ds(pl.multiple_of(c * CHUNK, CHUNK), CHUNK)


class Tiles:
    def __init__(self, peers, stat, sems):
        self.peers, self.stat, self.sems = peers, stat, sems

    def copy(self, k, c, owner):
        tile = self.stat.at[owner, c]
        return self.peers.copy(
            self.peers.to(k), tile, tile, self.sems[0].at[k - 1, c], self.sems[1].at[k - 1, c]
        )

    def start(self, c):
        for k in range(1, self.peers.count):
            self.copy(k, c, self.peers.me).start()

    def arrived(self, c):
        for k in range(1, self.peers.count):
            self.copy(k, c, self.peers.source(k)).wait_recv()

    def sent(self, c):
        for k in range(1, self.peers.count):
            self.copy(k, c, self.peers.me).wait_send()


class Gather:
    def __init__(self, peers, pay, sems):
        self.peers, self.pay, self.sems = peers, pay, sems

    def copy(self, way, hop, c, owner, which):
        slot = lax.rem(which, self.pay.shape[0])
        block = self.pay.at[slot, rows_of(c), self.peers.columns(owner)]
        device = jnp.clip(self.peers.me + (1 - 2 * way), 0, self.peers.count - 1)
        return self.peers.copy(
            device, block, block, self.sems[0].at[slot, way, hop - 1, c], self.sems[1].at[slot, way, hop - 1, c]
        )

    def onward(self, way):
        return self.peers.me < self.peers.count - 1 if way == 0 else self.peers.me > 0

    def owner(self, way, hop):
        return self.peers.me - hop if way == 0 else self.peers.me + hop

    def comes(self, way, hop):
        owner = self.owner(way, hop)
        return owner >= 0 if way == 0 else owner < self.peers.count

    def start(self, c, which):
        for way in (0, 1):
            @pl.when(self.onward(way))
            def _():
                self.copy(way, 1, c, self.peers.me, which).start()

    def relay(self, hop, c, which):
        for way in (0, 1):
            @pl.when(self.comes(way, hop))
            def _():
                self.copy(way, hop, c, self.owner(way, hop), which).wait_recv()
                if hop < self.peers.count - 1:
                    @pl.when(self.onward(way))
                    def _():
                        self.copy(way, hop + 1, c, self.owner(way, hop), which).start()

    def sent(self, c, which):
        for way in (0, 1):
            for hop in range(1, self.peers.count):
                @pl.when(self.comes(way, hop - 1) & self.onward(way))
                def _():
                    self.copy(way, hop, c, self.owner(way, hop - 1), which).wait_send()


class Scatter:
    def __init__(self, peers, part, stage, land, sems):
        self.peers, self.part, self.stage, self.land, self.sems = peers, part, stage, land, sems

    def landing(self, way, target, owner):
        if way == 0:
            return self.peers.columns(target)
        return self.peers.columns(jnp.where(target == owner, self.peers.count, target))

    def copy(self, way, c, target, which):
        slot, device = lax.rem(which, 2), jnp.clip(self.peers.me + (1 - 2 * way), 0, self.peers.count - 1)
        return self.peers.copy(
            device, self.stage.at[rows_of(c), self.peers.columns(target)],
            self.land.at[slot, rows_of(c), self.landing(way, target, device)],
            self.sems[0].at[slot, way, target, c], self.sems[1].at[slot, way, target, c],
        )

    def come(self, way, c, target, which):
        slot, columns = lax.rem(which, 2), self.landing(way, target, self.peers.me)
        block = self.land.at[slot, rows_of(c), columns]
        self.peers.copy(
            self.peers.me, block, block, self.sems[0].at[slot, way, target, c], self.sems[1].at[slot, way, target, c]
        ).wait_recv()
        return self.land[slot, rows_of(c), columns].astype(jnp.float32)

    def inward(self, way):
        return self.peers.me > 0 if way == 0 else self.peers.me < self.peers.count - 1

    def passes(self, way, target):
        return self.peers.me < target if way == 0 else self.peers.me > target

    def lag(self, way):
        return self.peers.me if way == 0 else self.peers.count - 1 - self.peers.me

    def push(self, way, c, which):
        rows = rows_of(c)
        targets = range(self.peers.count - 1, 0, -1) if way == 0 else range(self.peers.count - 1)
        for target in targets:
            columns = self.peers.columns(target)

            @pl.when(self.passes(way, target))
            def _():
                @pl.when(which > 0)
                def _():
                    self.copy(way, c, target, which - 1).wait_send()

                @pl.when(self.inward(way))
                def _():
                    self.stage[rows, columns] = (
                        self.part[rows, columns] + self.come(way, c, target, which)
                    ).astype(jnp.bfloat16)

                @pl.when(jnp.logical_not(self.inward(way)))
                def _():
                    self.stage[rows, columns] = self.part[rows, columns].astype(jnp.bfloat16)

                self.copy(way, c, target, which).start()

    def total(self, c, which):
        rows, mine = rows_of(c), self.peers.columns(self.peers.me)
        for way in (0, 1):
            @pl.when(self.inward(way))
            def _():
                self.part[rows, mine] += self.come(way, c, self.peers.me, which)
        return self.part[rows, mine]

    def sent(self, c, which):
        for target in range(self.peers.count):
            for way in (0, 1):
                @pl.when(self.passes(way, target))
                def _():
                    self.copy(way, c, target, which).wait_send()


def ticks_of(peers, chunks, passes, before, backward, begin, gather, compute, scatter):
    count = peers.count
    period = max(2 * count - 2, chunks + 1)

    def split(at):
        which, i = lax.div(at, period), lax.rem(at, period)
        chunk = chunks - 1 - i if backward else i
        return which, jnp.clip(chunk, 0, chunks - 1), (at >= 0) & (i < chunks) & (which < passes)

    def tick(t):
        which, c, there = split(t)
        last = (which == passes) & (lax.rem(t, period) < chunks)

        @pl.when(there | last)
        def _():
            begin(which, c)

        def relay(hop):
            moved, c_hop, there = split(t - hop)

            @pl.when(there)
            def _():
                gather.relay(hop, c_hop, moved + before)

        def push(middle):
            for way in (0, 1):
                lag = scatter.lag(way)
                moved, c_way, there = split(t - (count - 1) - lag)

                @pl.when(there & ((lag == 1) == middle))
                def _():
                    scatter.push(way, c_way, moved + before)

        relay(count - 1)
        which, c, there = split(t - (count - 1))

        @pl.when(there)
        def _():
            compute(which, c)

        push(False)
        for hop in range(1, count - 1):
            relay(hop)
        push(True)
    return tick


def mix_chunk(peers, c, pay, tiles, full_ref, mixed_ref, normal_ref, edge_ref, std_ref, last_ref):
    count, width = peers.count, peers.width
    tiles.arrived(c)
    columns = to_columns([tiles.stat[source, c] for source in range(count)])
    middles = [columns[:, SUB * source : SUB * source + 1] for source in range(count)]
    center = sum(middles) / count
    square = sum(columns[:, SUB * source + 1 : SUB * source + 2] for source in range(count))
    square = square + width * sum((middle - center) * (middle - center) for middle in middles)
    inv_std = lax.rsqrt(square / (count * width) + epsilon)
    std_ref[rows_of(c), :] = jnp.broadcast_to(inv_std, (CHUNK, LANES))
    for source in range(count):
        part = slice(source * width, (source + 1) * width)
        normal = (
            pay[rows_of(c), part].astype(jnp.float32) + (middles[source] - center)
        ) * inv_std
        normal_ref[rows_of(c), part] = normal.astype(jnp.bfloat16)
        normed = normal * full_ref[0:1, part] + full_ref[1:2, part]
        before = last_ref[0:1, part]
        edge_ref[pl.ds(c, 1), part] = before
        shifted = shift_rows(normed, before)
        last_ref[0:1, part] = normed[CHUNK - 1 : CHUNK]
        gap = normed - shifted
        for i in range(mixed_ref.shape[0]):
            mixed_ref[i, :, part] = (shifted + gap * full_ref[3 + i : 4 + i, part]).astype(
                jnp.bfloat16
            )


def wkv_join(left, right, fall):
    fallen = left[2] - fall
    peak = jnp.maximum(fallen, right[2])
    old, new = jnp.exp(fallen - peak), jnp.exp(right[2] - peak)
    return old * left[0] + new * right[0], old * left[1] + new * right[1], peak


def choose(mask, first, second):
    return tuple(jnp.where(mask, a, b) for a, b in zip(first, second))


def wkv_forward(base, key_ref, value_ref, decay, bonus, carry_ref, out_ref, state_ref):
    steps = STEP

    def at(s):
        return pl.ds(base + s * SUB, SUB)

    state = (value_ref[at(0), :], jnp.ones_like(decay), key_ref[at(0), :])
    for s in range(1, steps):
        key = key_ref[at(s), :]
        state = wkv_join(state, (value_ref[at(s), :], 1.0, key), decay)
    place = lax.broadcasted_iota(jnp.int32, decay.shape, 0)
    carry = tuple(carry_ref[i] for i in range(3))
    state = choose(place == 0, wkv_join(carry, state, steps * decay), state)
    for reach in (1, 2, 4):
        left = tuple(pltpu.roll(part, reach, 0) for part in state)
        state = choose(place >= reach, wkv_join(left, state, reach * steps * decay), state)
    after = tuple(pltpu.roll(part, 1, 0) for part in state)
    for i in range(3):
        carry_ref[i] = after[i]
    numer, denom, power = choose(place == 0, carry, after)
    for s in range(steps):
        key, value = key_ref[at(s), :], value_ref[at(s), :]
        lead = bonus + key
        peak = jnp.maximum(power, lead)
        old, new = jnp.exp(power - peak), jnp.exp(lead - peak)
        out_ref[at(s), :] = (old * numer + new * value) / (old * denom + new)
        state_ref[0, at(s), :] = numer
        state_ref[1, at(s), :] = denom
        state_ref[2, at(s), :] = power
        numer, denom, power = wkv_join((numer, denom, power), (value, 1.0, key), decay)


def wkv_backward(
    base, key_ref, value_ref, decay, bonus, out_ref, state_ref, up_ref, carry_ref, sum_ref, work_ref, grad_ref
):
    steps = STEP

    def at(s):
        return pl.ds(base + s * SUB, SUB)

    state = None
    for s in reversed(range(steps)):
        lead = bonus + key_ref[at(s), :]
        power = state_ref[2, at(s), :]
        peak = jnp.maximum(power, lead)
        new = jnp.exp(lead - peak)
        share = up_ref[s * SUB : (s + 1) * SUB, :] / (
            jnp.exp(power - peak) * state_ref[1, at(s), :] + new
        )
        work_ref[0, s], work_ref[1, s], work_ref[2, s] = share, peak, new * share
        here = (share, -share * out_ref[at(s), :], -peak)
        state = here if state is None else wkv_join(state, here, decay)
    place = lax.broadcasted_iota(jnp.int32, decay.shape, 0)
    carry = tuple(carry_ref[i] for i in range(3))
    state = choose(place == SUB - 1, wkv_join(carry, state, steps * decay), state)
    for reach in (1, 2, 4):
        later = tuple(pltpu.roll(part, SUB - reach, 0) for part in state)
        state = choose(place < SUB - reach, wkv_join(later, state, reach * steps * decay), state)
    after = tuple(pltpu.roll(part, SUB - 1, 0) for part in state)
    for i in range(3):
        carry_ref[i] = after[i]
    numer, denom, power = choose(place == SUB - 1, carry, after)
    for s in reversed(range(steps)):
        key, value, out = key_ref[at(s), :], value_ref[at(s), :], out_ref[at(s), :]
        share, peak, own = work_ref[0, s], work_ref[1, s], work_ref[2, s]
        reach = jnp.exp(key + power)
        direct = own * (value - out)
        grad_ref[0, s * SUB : (s + 1) * SUB, :] = direct + reach * (value * numer + denom)
        grad_ref[1, s * SUB : (s + 1) * SUB, :] = own + reach * numer
        sum_ref[1] += direct
        sum_ref[0] += jnp.exp(state_ref[2, at(s), :] + power - decay) * (
            state_ref[0, at(s), :] * numer + state_ref[1, at(s), :] * denom
        )
        numer, denom, power = wkv_join(
            (numer, denom, power), (share, -share * out, -peak), decay
        )


def load(pairs, sems, start):
    copies = [
        pltpu.make_async_copy(source, target, sems.at[start + i]) for i, (source, target) in enumerate(pairs)
    ]
    for copy in copies:
        copy.start()
    return copies


def soft_plus(value):
    small = jnp.exp(-jnp.abs(value))
    share = 1.0 / (1.0 + small)
    rest = jnp.where(small < 1e-3, small - 0.5 * small * small, jnp.log(1.0 + small))
    return jnp.maximum(value, 0.0) + rest, jnp.where(value >= 0.0, share, small * share)


def from_tokens(tokens_hbm, micro, tokens_ref, sems):
    return [
        pltpu.make_async_copy(tokens_hbm.at[micro, 0, :, pl.ds(g * LANES, LANES)], tokens_ref.at[g], sems.at[g])
        for g in range(tokens_ref.shape[0])
    ]


def to_sections(sections, rows_ref, tokens_ref, out_hbm, sems):
    send, receive = sems
    micro = lax.axis_index("section")
    groups = range(tokens_ref.shape[0])

    def ends(c, source, g):
        return tokens_ref.at[g, rows_of(c)], out_hbm.at[source, 0, :, pl.ds(g * LANES, LANES)]

    def copy(c, source, g):
        held, target = ends(c, source, g)
        return pltpu.make_async_remote_copy(
            src_ref=held, dst_ref=target, send_sem=send.at[c, g], recv_sem=receive.at[source, g],
            device_id={"section": c}, device_id_type=MESH,
        )

    def own(g):
        return pltpu.make_async_copy(*ends(micro, micro, g), send.at[micro, g])

    def start(c):
        to_tokens(rows_ref, tokens_ref, c)

        @pl.when(c == micro)
        def _():
            for g in groups:
                own(g).start()

        @pl.when(c != micro)
        def _():
            for g in groups:
                copy(c, micro, g).start()

    def wait():
        for g in groups:
            for k in range(1, sections):
                other = lax.rem(micro + k, sections)
                copy(other, micro, g).wait_send()
                copy(other, other, g).wait_recv()
            own(g).wait()

    return start, wait


def mix_chunk_back(
    peers, c, ratios, full_ref, normal_ref, edge_ref, mixed_ref, mix_grad, later_ref, edges_ref, part_ref, tiles
):
    count = peers.count
    rows = rows_of(c)
    first = second = 0.0
    for source in range(count):
        part = peers.columns(source)
        normal = normal_ref[rows, part].astype(jnp.float32)
        gain = full_ref[0:1, part]
        normed = normal * gain + full_ref[1:2, part]
        before = shift_rows(normed, edge_ref[pl.ds(c, 1), part])
        gap = normed - before
        direct = shifted = 0.0
        for i in range(ratios):
            grad = mix_grad(i, part)
            ratio = full_ref[3 + i : 4 + i, part]
            mixed_ref[i, rows, part] = (before + gap * ratio).astype(jnp.bfloat16)
            taken = grad * ratio
            direct = direct + taken
            shifted = shifted + (grad - taken)
            edges_ref[3 + i : 4 + i, part] += jnp.sum(grad * gap, axis=0, keepdims=True)
        value = direct + unshift_rows(shifted, later_ref[0:1, part])
        later_ref[0:1, part] = shifted[0:1]
        part_ref[rows, part] = value
        scaled = value * gain
        first = first + jnp.sum(scaled, axis=1, keepdims=True)
        second = second + jnp.sum(scaled * normal, axis=1, keepdims=True)
    tiles.stat[peers.me, c] = to_row_tile(first, second)
    tiles.start(c)


STEPS = 7
COPIES = 21


class Summed:
    def __init__(self, grad, core_land, cross_land, own_land, result, sems):
        self.grad, self.core_land, self.cross_land, self.own_land = grad, core_land, cross_land, own_land
        self.result, self.sems = result, sems
        self.rows = grad.shape[-2]
        self.half, self.piece, self.sub = self.rows // 2, self.rows // 8, self.rows // 16
        self.q, self.s = lax.axis_index("seq"), lax.axis_index("section")
        self.y, self.x = lax.div(self.s, 2), lax.rem(self.s, 2)
        self.sibling = {"seq": 1 - self.q}
        self.over_x = {"section": self.s + 1 - 2 * self.x}
        self.over_y = {"section": self.s + 2 - 4 * self.y}

    def at(self, ref, start, size):
        return ref.at[pl.ds(pl.multiple_of(start, 16), size), :]

    def spot(self, q, y, x, part):
        return q * self.half + (2 * y + x) * self.piece + part * self.sub

    def send(self, which, source, target, place):
        return pltpu.make_async_remote_copy(
            src_ref=source, dst_ref=target, send_sem=self.sems[0].at[which], recv_sem=self.sems[1].at[which],
            device_id=place, device_id_type=MESH,
        )

    def add(self, start, land, land_start, size):
        columns = self.grad.shape[-1]
        block = min(size, max(16, 32768 // columns))

        def step(i, unused):
            mine = self.at(self.grad, start + i * block, block)
            come = self.at(land, land_start + i * block, block)
            mine[...] = (mine[...].astype(jnp.float32) + come[...].astype(jnp.float32)).astype(jnp.bfloat16)
            return unused

        lax.fori_loop(0, size // block, step, 0)

    def to_core(self):
        other = self.at(self.grad, (1 - self.q) * self.half, self.half)
        return [self.send(0, other, self.core_land, self.sibling)]

    def cross(self, y, x):
        out = []
        for k in (0, 1):
            for part, place, (py, px) in (
                (0, self.over_x, (k, 1 - x)), (1, self.over_y, (1 - y, k)),
            ):
                spot = self.spot(0, py, px, part)
                out.append(
                    self.send(
                        1 + 2 * k + part, self.at(self.grad, self.q * self.half + spot, self.sub),
                        self.at(self.cross_land, spot, self.sub), place,
                    )
                )
        return out

    def own(self):
        out = []
        for part, place, (py, px) in (
            (0, self.over_y, (1 - self.y, self.x)), (1, self.over_x, (self.y, 1 - self.x)),
        ):
            source = self.at(self.grad, self.spot(self.q, py, px, part), self.sub)
            out.append(self.send(5 + part, source, self.at(self.own_land, part * self.sub, self.sub), place))
        return out

    def share(self, which, q, y, x, part, size, place, held):
        spot = self.spot(q, y, x, part)
        return self.send(which, self.at(held, spot, size), self.at(self.result, spot, size), place)

    def back_own(self, q, y, x):
        return [
            self.share(7, q, y, x, 0, self.sub, self.over_y, self.grad),
            self.share(8, q, y, x, 1, self.sub, self.over_x, self.grad),
            self.share(9, q, y, x, 0, self.piece, self.sibling, self.grad),
        ]

    def back_cross(self):
        q, y, x = self.q, self.y, self.x
        return [
            self.share(10, q, y, x, 0, self.sub, self.over_x, self.result),
            self.share(11, q, 1 - y, x, 0, self.sub, self.over_x, self.result),
            self.share(12, q, y, x, 1, self.sub, self.over_y, self.result),
            self.share(13, q, y, 1 - x, 1, self.sub, self.over_y, self.result),
            self.share(14, q, 1 - y, x, 0, self.sub, self.sibling, self.result),
            self.share(15, q, y, 1 - x, 1, self.sub, self.sibling, self.result),
        ]

    def back_core(self):
        q, y, x = self.q, self.y, self.x
        return [
            self.share(16, q, y, 1 - x, 0, self.sub, self.sibling, self.result),
            self.share(17, q, 1 - y, 1 - x, 0, self.sub, self.sibling, self.result),
            self.share(18, q, 1 - y, x, 1, self.sub, self.sibling, self.result),
            self.share(19, q, 1 - y, 1 - x, 1, self.sub, self.sibling, self.result),
        ]

    def keep(self):
        spot = self.spot(self.q, self.y, self.x, 0)
        return pltpu.make_async_copy(
            self.at(self.grad, spot, self.piece), self.at(self.result, spot, self.piece), self.sems[0].at[20]
        )

    def arrive(self, which, ref, start, size):
        view = self.at(ref, start, size)
        self.send(which, view, view, self.sibling).wait_recv()

    def step(self, number):
        q, y, x = self.q, self.y, self.x
        if number == 0:
            started = self.to_core()
        elif number == 1:
            self.arrive(0, self.core_land, 0, self.half)
            self.add(q * self.half, self.core_land, 0, self.half)
            started = self.cross(y, x)
        elif number == 2:
            for k in (0, 1):
                for part, (py, px) in ((0, (k, x)), (1, (y, k))):
                    spot = self.spot(0, py, px, part)
                    self.arrive(1 + 2 * k + part, self.cross_land, spot, self.sub)
                    self.add(q * self.half + spot, self.cross_land, spot, self.sub)
            started = self.own()
        elif number == 3:
            for part in (0, 1):
                self.arrive(5 + part, self.own_land, part * self.sub, self.sub)
                self.add(self.spot(q, y, x, part), self.own_land, part * self.sub, self.sub)
            started = self.back_own(q, y, x) + [self.keep()]
        elif number == 4:
            self.arrive(7, self.result, self.spot(q, 1 - y, x, 0), self.sub)
            self.arrive(8, self.result, self.spot(q, y, 1 - x, 1), self.sub)
            self.keep().wait()
            started = self.back_cross()
        elif number == 5:
            self.arrive(9, self.result, self.spot(1 - q, y, x, 0), self.piece)
            self.arrive(10, self.result, self.spot(q, y, 1 - x, 0), self.sub)
            self.arrive(11, self.result, self.spot(q, 1 - y, 1 - x, 0), self.sub)
            self.arrive(12, self.result, self.spot(q, 1 - y, x, 1), self.sub)
            self.arrive(13, self.result, self.spot(q, 1 - y, 1 - x, 1), self.sub)
            started = self.back_core()
        else:
            o = 1 - q
            self.arrive(14, self.result, self.spot(o, 1 - y, x, 0), self.sub)
            self.arrive(15, self.result, self.spot(o, y, 1 - x, 1), self.sub)
            self.arrive(16, self.result, self.spot(o, y, 1 - x, 0), self.sub)
            self.arrive(17, self.result, self.spot(o, 1 - y, 1 - x, 0), self.sub)
            self.arrive(18, self.result, self.spot(o, 1 - y, x, 1), self.sub)
            self.arrive(19, self.result, self.spot(o, 1 - y, 1 - x, 1), self.sub)
            started = []
        for copy in started:
            copy.start()

    def sent_grad(self):
        copies = self.to_core() + self.cross(self.y, self.x) + self.own() + self.back_own(self.q, self.y, self.x)
        for copy in copies:
            copy.wait_send()

    def sent_rest(self):
        for copy in self.back_cross() + self.back_core():
            copy.wait_send()


GROUPS = (
    (0, (1,), (1, 2, 4, 5, 6, 11)),
    (0, (0, 2), (0, 1, 3, 4, 5, 11)),
    (1, (3, 4, 5, 6), (1, 2, 4, 5, 6, 12)),
)


def both_kernel(
    count, sections, cores, depth,
    rows_hbm, up_hbm, lead_ref, numer_ref, denom_ref, power_ref, attend_gain, attend_bias, attend_mix, fading_ref, bonus_ref,
    feed_gain, feed_bias, feed_mix, entry_hbm, exit_hbm, key_hbm, content_hbm, gate_hbm,
    out_hbm, back_hbm, table_ref, entry_sum, exit_sum, key_sum, content_sum, gate_sum,
    normal_ref, std_ref, key_ref, value_ref, averaged_ref, state_ref, open_ref, hidden_ref, slope_ref, gate_ref, kv_ref,
    full_ref, edge_ref, rows_ref, tokens_ref, grad_ref, back_ref,
    entry_ref, exit_ref, w_key, w_content, w_gate,
    entry_grad, exit_grad, key_grad, content_grad, gate_grad,
    entry_core, exit_core, key_core, content_core, gate_core,
    entry_cross, exit_cross, key_cross, content_cross, gate_cross,
    entry_own, exit_own, key_own, content_own, gate_own,
    pay, stat, part, stage, land, mixed_ref, pre_grads, up_ref, work_ref, pair_ref, carry_ref, sum_ref,
    output_ref, hidden_grad, last_ref, later_ref, edges_ref, edge_land, small_ref,
    load_sems, token_sems, back_sems, fs, fr, os, orr, bs, br, gs, gr, ts, tr, ss, sr, es, er, ws, wr,
    table_send, table_recv,
):
    length, width = rows_ref.shape
    hidden_width = hidden_ref.shape[2]
    chunks = length // CHUNK
    passes = 2 * depth
    period = max(2 * count - 2, chunks + 1)
    peers = Peers(count, width)
    mine = peers.columns(peers.me)
    micro, core = lax.axis_index("section"), lax.axis_index("seq")
    first = from_tokens(rows_hbm, micro, tokens_ref, token_sems)
    second = from_tokens(up_hbm, micro, back_ref, back_sems)
    for copy in first + second:
        copy.start()
    weights = load(
        (
            (entry_hbm, entry_ref), (exit_hbm, exit_ref), (key_hbm, w_key), (content_hbm, w_content),
            (gate_hbm, w_gate),
        ),
        load_sems,
        0,
    )
    full_ref[...] = jnp.zeros_like(full_ref)
    for j in range(2 * depth):
        level = j // 2
        gain, bias, mix = (attend_gain, attend_bias, attend_mix) if j % 2 == 0 else (feed_gain, feed_bias, feed_mix)
        full_ref[j, 0:1, mine] = gain[level : level + 1, :]
        full_ref[j, 1:2, mine] = bias[level : level + 1, :]
        full_ref[j, 2:3, mine] = lead_ref[j, micro]
        full_ref[j, 3 : 3 + mix.shape[1], mine] = mix[level]
    gather = Gather(peers, pay, (gs, gr))
    tiles = Tiles(peers, stat, (ts, tr))
    scatter = Scatter(peers, part, stage, land, (ss, sr))
    start_out, wait_out = to_sections(sections, rows_ref, tokens_ref, out_hbm, (os, orr))
    start_back, wait_back = to_sections(sections, grad_ref, back_ref, back_hbm, (bs, br))

    def full_copy(k, owner):
        block = full_ref.at[:, :, peers.columns(owner)]
        return peers.copy(peers.to(k), block, block, fs.at[k - 1], fr.at[k - 1])

    def sums(group, level):
        parts = (
            (key_grad, key_core, key_cross, key_own, key_sum),
            (content_grad, content_core, content_cross, content_own, content_sum),
            (gate_grad, gate_core, gate_cross, gate_own, gate_sum),
        )
        entry = (entry_grad, entry_core, entry_cross, entry_own, entry_sum)
        parts += tuple(
            (*(ref.at[i] for ref in entry[:4]), entry_sum.at[:, i]) for i in range(3)
        )
        parts += ((exit_grad, exit_core, exit_cross, exit_own, exit_sum),)
        out = []
        for place in GROUPS[group][1]:
            grad, core_land, cross_land, own_land, result = parts[place]
            out.append(
                Summed(
                    grad, core_land, cross_land, own_land, result.at[level],
                    (ws.at[level, place], wr.at[level, place]),
                )
            )
        return out

    def sum_step(group, level, number):
        for matrix in sums(group, level):
            matrix.step(number)

    def table_place(k):
        return lax.rem(micro * cores + core + k, sections * cores)

    def table_copy(k, owner):
        other = table_place(k)
        return pltpu.make_async_remote_copy(
            src_ref=small_ref, dst_ref=table_ref.at[owner], send_sem=table_send.at[k - 1], recv_sem=table_recv.at[k - 1],
            device_id={"section": lax.div(other, cores), "seq": lax.rem(other, cores)}, device_id_type=MESH,
        )

    others = [table_place(k) for k in range(1, sections * cores)]
    peers.greet([{"section": lax.div(other, cores), "seq": lax.rem(other, cores)} for other in others])
    for k in range(1, count):
        full_copy(k, peers.me).start()
    for copy in first:
        copy.wait()
    to_stretches(tokens_ref, rows_ref)

    def begin_forward(j, c):
        rows = rows_of(c)

        @pl.when(j > 0)
        def _():
            value = scatter.total(c, j - 1)
            tiles.sent(c)

            @pl.when(lax.rem(j, 2) == 1)
            def _():
                rows_ref[rows, :] += value

            @pl.when(lax.rem(j, 2) == 0)
            def _():
                level = lax.div(j, 2) - 1
                kv_ref[level, rows, :] = value
                rows_ref[rows, :] += gate_ref[level, rows, :] * value

        @pl.when(j < 2 * depth)
        def _():
            lines = rows_ref[rows, :]
            middle = jnp.mean(lines, axis=1, keepdims=True)
            center = lines - middle
            square = jnp.sum(center * center, axis=1, keepdims=True)
            pay[lax.rem(j, 2), rows, mine] = center.astype(jnp.bfloat16)
            tiles.stat[peers.me, c] = to_row_tile(middle, square)
            tiles.start(c)
            gather.start(c, j)

        @pl.when(j == 2 * depth)
        def _():
            start_out(c)

    def attend_forward(level, c):
        rows = rows_of(c)

        @pl.when(c == 0)
        def _():
            for i, start_ref in enumerate((numer_ref, denom_ref, power_ref)):
                carry_ref[i] = jnp.broadcast_to(start_ref[level, micro], (SUB, width))

        decay = jnp.broadcast_to(jnp.exp(fading_ref[pl.ds(level, 1), :]), (SUB, width))
        bonus = jnp.broadcast_to(bonus_ref[pl.ds(level, 1), :], (SUB, width))
        key_ref[level, rows, :] = product(mixed_ref[0, 0:CHUNK], entry_ref[level, 0])
        value_ref[level, rows, :] = product(mixed_ref[1, 0:CHUNK], entry_ref[level, 1])
        gate = jax.nn.sigmoid(product(mixed_ref[2, 0:CHUNK], entry_ref[level, 2]))
        open_ref[level, rows, :] = gate
        wkv_forward(
            pl.multiple_of(c * CHUNK, CHUNK), key_ref.at[level], value_ref.at[level], decay, bonus, carry_ref,
            averaged_ref.at[level], state_ref.at[level],
        )
        output = (gate * averaged_ref[level, rows, :]).astype(jnp.bfloat16)
        for target in range(count):
            block = peers.columns(target)
            part[rows, block] = product(output, exit_ref[level, :, block])

    def feed_forward(level, c):
        rows = rows_of(c)
        for start in range(0, hidden_ref.shape[2], width):
            block = slice(start, start + width)
            soft, slope = soft_plus(product(mixed_ref[0, 0:CHUNK], w_key[level, :, block]))
            hidden_ref[level, rows, block] = (soft * soft).astype(jnp.bfloat16)
            slope_ref[level, rows, block] = (2.0 * soft * slope).astype(jnp.bfloat16)
        for target in range(count):
            block = peers.columns(target)
            part[rows, block] = product(hidden_ref[level, rows, :], w_content[level, :, block])
        gate_ref[level, rows, :] = jax.nn.sigmoid(product(mixed_ref[1, 0:CHUNK], w_gate[level]))

    def forward(j, c):
        @pl.when((j == 0) & (c == 0))
        def _():
            for k in range(1, count):
                full_copy(k, peers.source(k)).wait_recv()
            for copy in weights:
                copy.wait()

        @pl.when(c == 0)
        def _():
            last_ref[0:1, :] = full_ref[j, 2:3, :]

        mix_chunk(
            peers, c, pay.at[lax.rem(j, 2)], tiles, full_ref.at[j], mixed_ref.at[:, pl.ds(0, CHUNK)], normal_ref.at[j], edge_ref.at[j], std_ref.at[j],
            last_ref,
        )
        level = lax.div(j, 2)

        @pl.when(lax.rem(j, 2) == 0)
        def _():
            attend_forward(level, c)

        @pl.when(lax.rem(j, 2) == 1)
        def _():
            feed_forward(level, c)

        gather.sent(c, j)

    def edge_copies(j, source_of):
        return [
            peers.copy(
                peers.to(k), edges_ref.at[j, :, peers.columns(peers.to(k))], edge_land.at[j, source_of(k)],
                es.at[j, k - 1], er.at[j, k - 1],
            )
            for k in range(1, count)
        ]

    def end_pass(j, c):
        rows = rows_of(c)
        normed_grad = scatter.total(c, 2 * passes - 1 - j)
        tiles.arrived(c)
        totals = tiles.stat[0, c]
        for source in range(1, count):
            totals = totals + tiles.stat[source, c]
        columns = to_columns([totals])
        normal = normal_ref[j, rows, mine].astype(jnp.float32)
        scale = 1.0 / (count * width)
        grad_ref[rows, :] += std_ref[j, rows, 0:1] * (
            normed_grad * full_ref[j, 0:1, mine] - columns[:, 0:1] * scale - normal * (columns[:, 1:2] * scale)
        )
        small_ref[j, 0:1, :] += jnp.sum(normed_grad * normal, axis=0, keepdims=True)
        small_ref[j, 1:2, :] += jnp.sum(normed_grad, axis=0, keepdims=True)

        @pl.when(c == 0)
        def _():
            for copy in edge_copies(j, peers.source):
                copy.wait_recv()
            edges = edges_ref[j, :, mine]
            for k in range(1, count):
                edges = edges + edge_land[j, peers.source(k)]
            small_ref[j, 2:6, :] = edges[2:6]

    def begin_backward(which, c):
        rows = rows_of(c)
        j = passes - 1 - which

        @pl.when(which > 0)
        def _():
            end_pass(j + 1, c)
            gather.sent(c, passes + which - 1)
            tiles.sent(c)

        @pl.when((which < passes) & (lax.rem(which, 2) == 0))
        def _():
            pay[lax.rem(which, 2), rows, mine] = (grad_ref[rows, :] * gate_ref[lax.div(j, 2), rows, :]).astype(jnp.bfloat16)

        @pl.when((which < passes) & (lax.rem(which, 2) == 1))
        def _():
            pay[lax.rem(which, 2), rows, mine] = grad_ref[rows, :].astype(jnp.bfloat16)

        @pl.when(which < passes)
        def _():
            gather.start(c, passes + which)

        @pl.when(which == passes)
        def _():
            start_back(c)

    def attend_backward(j, c):
        level = lax.div(j, 2)
        rows = rows_of(c)
        decay = jnp.broadcast_to(jnp.exp(fading_ref[pl.ds(level, 1), :]), (SUB, width))
        bonus = jnp.broadcast_to(bonus_ref[pl.ds(level, 1), :], (SUB, width))

        @pl.when(c == chunks - 1)
        def _():
            sum_ref[...] = jnp.zeros_like(sum_ref)
            carry_ref[0] = jnp.zeros((SUB, width), jnp.float32)
            carry_ref[1] = jnp.zeros((SUB, width), jnp.float32)
            carry_ref[2] = jnp.full((SUB, width), NO_POWER, jnp.float32)

        output_grad = against(pay[1, rows, :], exit_ref[level])
        gate = open_ref[level, rows, :]
        up = output_grad * gate
        up_ref[...] = up
        averaged = averaged_ref[level, rows, :]
        pre_grads[2, rows, :] = (up * averaged * (1.0 - gate)).astype(jnp.bfloat16)
        output_ref[rows, :] = (gate * averaged).astype(jnp.bfloat16)
        wkv_backward(
            pl.multiple_of(c * CHUNK, CHUNK), key_ref.at[level], value_ref.at[level], decay, bonus,
            averaged_ref.at[level], state_ref.at[level],
            up_ref, carry_ref, sum_ref, work_ref, pair_ref,
        )
        pre_grads[0, rows, :] = pair_ref[0].astype(jnp.bfloat16)
        pre_grads[1, rows, :] = pair_ref[1].astype(jnp.bfloat16)
        mix_chunk_back(
            peers, c, 3, full_ref.at[j], normal_ref.at[j], edge_ref.at[j], mixed_ref,
            lambda i, columns: against(pre_grads[i, rows, :], entry_ref[level, i, columns, :]),
            later_ref, edges_ref.at[j], part, tiles,
        )

        @pl.when(c == 0)
        def _():
            numer, denom = carry_ref[0, SUB - 1 :, :], carry_ref[1, SUB - 1 :, :]
            lift = jnp.exp(power_ref[level, micro] + carry_ref[2, SUB - 1 :, :])
            out = passes + level
            small_ref[out, 0:1, :] = -decay[0:1] * jnp.sum(sum_ref[0], axis=0, keepdims=True)
            small_ref[out, 1:2, :] = jnp.sum(sum_ref[1], axis=0, keepdims=True)
            small_ref[out, 2:3, :] = lift * numer
            small_ref[out, 3:4, :] = lift * denom
            small_ref[out, 4:5, :] = lift * (numer_ref[level, micro] * numer + denom_ref[level, micro] * denom)

    def feed_backward(j, c):
        rows = rows_of(c)
        level = lax.div(j, 2)
        gate = gate_ref[level, rows, :]
        pre_grads[0, rows, :] = (grad_ref[rows, :] * gate * kv_ref[level, rows, :] * (1.0 - gate)).astype(jnp.bfloat16)
        for start in range(0, hidden_width, width):
            block = slice(start, start + width)
            into = against(pay[0, rows, :], w_content[level, block, :])
            hidden_grad[rows, block] = (into * slope_ref[level, rows, block].astype(jnp.float32)).astype(jnp.bfloat16)

        def mix_grad(i, columns):
            if i == 0:
                return against(hidden_grad[rows, :], w_key[level, columns, :])
            return against(pre_grads[0, rows, :], w_gate[level, columns, :])

        mix_chunk_back(
            peers, c, 2, full_ref.at[j], normal_ref.at[j], edge_ref.at[j], mixed_ref, mix_grad,
            later_ref, edges_ref.at[j], part, tiles,
        )

    def backward(which, c):
        j = passes - 1 - which

        @pl.when(c == chunks - 1)
        def _():
            later_ref[...] = jnp.zeros_like(later_ref)

        @pl.when(lax.rem(which, 2) == 0)
        def _():
            feed_backward(j, c)

        @pl.when(lax.rem(which, 2) == 1)
        def _():
            attend_backward(j, c)

        @pl.when(c == 0)
        def _():
            edges_ref[j, 2:3, :] = later_ref[0:1, :]
            for copy in edge_copies(j, lambda k: peers.me):
                copy.start()

    def weigh(place, level):
        for source in range(count):
            block = peers.columns(source)
            if place == 0:
                key_grad[block, :] = inner_rows(mixed_ref[0, :, block], hidden_grad[...]).astype(jnp.bfloat16)
            elif place == 2:
                gate_grad[block, :] = inner_rows(mixed_ref[1, :, block], pre_grads[0]).astype(jnp.bfloat16)
            elif 3 <= place < 6:
                i = place - 3
                entry_grad[i, block, :] = inner_rows(mixed_ref[i, :, block], pre_grads[i]).astype(jnp.bfloat16)
            elif place == 6:
                exit_grad[:, block] = inner_rows(output_ref[...], pay[1, :, block]).astype(jnp.bfloat16)
        if place == 1:
            for start in range(0, hidden_width, width):
                block = slice(start, start + width)
                content_grad[block, :] = inner_rows(hidden_ref[level, :, block], pay[0]).astype(jnp.bfloat16)

    base, final = chunks + count - 1, passes * period + chunks - 1

    def when_taken(group, number, t):
        kind, places, later = GROUPS[group]
        since = t - (base + period * kind + later[number])
        taken = (since >= 0) & (lax.rem(since, 2 * period) == 0) & (since < 2 * period * depth)
        return taken, depth - 1 - lax.div(since, 2 * period)

    def extra(t):
        for group in range(len(GROUPS)):
            for number in reversed(range(STEPS - 1)):
                taken, level = when_taken(group, number, t)

                @pl.when(taken)
                def _():
                    if number == 0:
                        @pl.when(level < depth - 1)
                        def _():
                            for matrix in sums(group, jnp.minimum(level + 1, depth - 1)):
                                matrix.sent_grad()

                        for place in GROUPS[group][1]:
                            weigh(place, jnp.clip(level, 0, depth - 1))
                    sum_step(group, jnp.clip(level, 0, depth - 1), number)

    forward_tick = ticks_of(peers, chunks, passes, 0, False, begin_forward, gather, forward, scatter)
    backward_tick = ticks_of(peers, chunks, passes, passes, True, begin_backward, gather, backward, scatter)
    turn = (passes - 1) * period + chunks + count - 1

    def tick(t, unused):
        @pl.when(t < passes * period + chunks)
        def _():
            forward_tick(t)

        @pl.when(t == turn - 1)
        def _():
            for copy in second:
                copy.wait()
            to_stretches(back_ref, grad_ref)
            small_ref[...] = jnp.zeros_like(small_ref)
            edges_ref[...] = jnp.zeros_like(edges_ref)

        @pl.when(t >= turn)
        def _():
            backward_tick(t - turn)
            extra(t - turn)

        return unused

    lax.fori_loop(0, turn + final + 1, tick, 0)

    for k in range(1, sections * cores):
        table_copy(k, micro * cores + core).start()
    table_ref[micro * cores + core] = small_ref[...]
    left = []
    for group, (kind, places, later) in enumerate(GROUPS):
        for level in reversed(range(depth)):
            start = base + period * (kind + 2 * (depth - 1 - level))
            for number in range(STEPS):
                at = start + (later[number] if number < STEPS - 1 else later[-1] + 5)
                if at > final or number == STEPS - 1:
                    left.append((at, group, level, number))
    for at, group, level, number in sorted(left):
        sum_step(group, level, number)
    for c in range(chunks):
        scatter.sent(c, 2 * passes - 1)
    for j in range(passes):
        for copy in edge_copies(j, lambda k: peers.me):
            copy.wait_send()
    for group in range(len(GROUPS)):
        for level in range(depth):
            for matrix in sums(group, level):
                matrix.sent_rest()
                if level == 0:
                    matrix.sent_grad()
    for k in range(1, sections * cores):
        table_copy(k, micro * cores + core).wait_send()
        other = lax.rem(micro * cores + core + sections * cores - k, sections * cores)
        table_copy(k, other).wait_recv()
    for k in range(1, count):
        full_copy(k, peers.me).wait_send()
    wait_out()
    wait_back()


BF16, F32 = jnp.bfloat16, jnp.float32


def struct(*shape, dtype=F32):
    return jax.ShapeDtypeStruct(shape, dtype)


def run_kernel(body, collective, outs, scratch, operands, flops):
    def spec(inside):
        return pl.BlockSpec(memory_space=pltpu.VMEM if inside else pl.ANY)

    return pl.pallas_call(
        body,
        out_shape=[out for out, inside in outs],
        in_specs=[spec(inside) for operand, inside in operands],
        out_specs=[spec(inside) for out, inside in outs],
        scratch_shapes=scratch,
        compiler_params=pltpu.CompilerParams(
            collective_id=collective, has_side_effects=True, vmem_limit_bytes=63 * 1024 * 1024
        ),
        cost_estimate=pl.CostEstimate(flops=flops, bytes_accessed=2**25, transcendentals=2**23),
    )(*[operand for operand, inside in operands])


def pair_of(shape):
    return [pltpu.SemaphoreType.DMA(shape)] * 2


def run_fast(
    residual_entering, upstream_sensitivity, piece_lead_lines, dividend_start, divisor_start, power_offset_start,
    attend_standard_scale, attend_standard_offset, attend_lag_fractions, fading_log_rate, reward_first_word,
    attend_entry_matrix, attend_exit_matrix, feed_standard_scale, feed_standard_offset, feed_lag_fractions,
    feed_lookup_matrix, feed_content_matrix, feed_gate_matrix,
):
    count, sections, cores = (lax.axis_size(axis) for axis in ("tp", "section", "seq"))
    length, width = residual_entering.shape[2:]
    depth, features, hidden = feed_lookup_matrix.shape[0], count * width, feed_lookup_matrix.shape[2]
    chunks, subs = length // CHUNK, 2 * depth
    flops = 2 * depth * length * features * (4 * width + 2 * hidden + width)
    groups = width // LANES
    starts = (dividend_start, divisor_start, power_offset_start)
    weights = (attend_entry_matrix, attend_exit_matrix, feed_lookup_matrix, feed_content_matrix, feed_gate_matrix)
    shares = struct(sections, 1, CHUNK, width)
    lines = (depth, length, width)
    shapes = [weight.shape[1:] for weight in weights]

    def held(*shape, dtype=F32):
        return pltpu.VMEM(shape, dtype)

    def rows_cut(by):
        return [held(*shape[:-2], shape[-2] // by, shape[-1], dtype=BF16) for shape in shapes]

    outs = [(shares, False), (shares, False), (struct(sections * cores, subs + depth, SUB, width), True)]
    outs += [(struct(*weight.shape, dtype=BF16), False) for weight in weights]
    scratch = [held(subs, length, features, dtype=BF16), held(subs, length, LANES), held(*lines), held(*lines)]
    scratch += [held(*lines), held(depth, 3, *lines[1:]), held(*lines)]
    scratch += [held(depth, length, hidden, dtype=BF16)] * 2 + [held(*lines)] * 2
    scratch += [held(subs, SUB, features)] * 2 + [held(length, width), held(groups, length, LANES)] * 2
    scratch += [held(*weight.shape, dtype=BF16) for weight in weights] + rows_cut(1) + rows_cut(2) + rows_cut(2) + rows_cut(8)
    scratch += [
        held(2, length, features, dtype=BF16), held(count, chunks, SUB, LANES), held(length, features),
        held(length, features, dtype=BF16), held(2, length, features + width, dtype=BF16),
    ]
    scratch += [
        held(3, length, features, dtype=BF16), held(3, length, width, dtype=BF16), held(CHUNK, width),
        held(3, STEP, SUB, width), held(2, CHUNK, width), held(3, SUB, width), held(2, SUB, width),
        held(length, width, dtype=BF16), held(length, hidden, dtype=BF16), held(SUB, features), held(SUB, features),
        held(subs, SUB, features), held(subs, count, SUB, width), held(subs + depth, SUB, width),
    ]
    scratch += [pltpu.SemaphoreType.DMA((n,)) for n in (len(weights), groups, groups)] + pair_of((count - 1,))
    scratch += pair_of((sections, groups)) + pair_of((sections, groups))
    scratch += pair_of((2, 2, count - 1, chunks)) + pair_of((count - 1, chunks)) + pair_of((2, 2, count, chunks))
    scratch += pair_of((subs, count - 1)) + pair_of((depth, len(weights) + 2, COPIES))
    scratch += pair_of((sections * cores - 1,))
    operands = [(residual_entering, False), (upstream_sensitivity, False)]
    operands += [
        (value, True)
        for value in (
            piece_lead_lines, *starts, attend_standard_scale, attend_standard_offset, attend_lag_fractions,
            fading_log_rate, reward_first_word, feed_standard_scale, feed_standard_offset, feed_lag_fractions,
        )
    ]
    operands += [(value, False) for value in weights]
    out_share, back_share, table, *sums = run_kernel(
        partial(both_kernel, count, sections, cores, depth), 0, outs, scratch, operands, 3 * flops
    )
    return finish(cores, depth, out_share, back_share, table, sums)


def finish_kernel(cores, depth, table_ref, *refs):
    wide, narrow = refs[:7], refs[7:14]
    prev, numer, denom, power = refs[14:18]
    attend_gain, attend_bias, attend_mix, decay, bonus, feed_gain, feed_bias, feed_mix = refs[18:]
    for source, target in zip(wide, narrow):
        target[...] = source[...].astype(jnp.float32)

    @pl.when(pl.program_id(0) == 0)
    def _():
        core = lax.axis_index("seq")
        places, subs = table_ref.shape[0], 2 * depth
        for m in range(places // cores):
            for j in range(subs):
                prev[j, m] = table_ref[m * cores + core, j, 2:3, :]
            for level in range(depth):
                for i, state in enumerate((numer, denom, power)):
                    state[level, m] = table_ref[m * cores + core, subs + level, 2 + i : 3 + i, :]
        for level in range(depth):
            for j, gain, bias, mix in (
                (2 * level, attend_gain, attend_bias, attend_mix), (2 * level + 1, feed_gain, feed_bias, feed_mix),
            ):
                total = sum(table_ref[place, j] for place in range(places))
                gain[level : level + 1, :] = total[0:1]
                bias[level : level + 1, :] = total[1:2]
                mix[level] = total[3 : 3 + mix.shape[1]]
            total = sum(table_ref[place, subs + level] for place in range(places))
            decay[level : level + 1, :] = total[0:1]
            bonus[level : level + 1, :] = total[1:2]


def finish(cores, depth, out_share, back_share, table, sums):
    steps = 8
    wide = [value.reshape(-1, value.shape[-1]) for value in (out_share, back_share, *sums)]
    blocks = [
        pl.BlockSpec((value.shape[0] // steps, value.shape[1]), lambda i: (i, 0)) for value in wide
    ]
    width = table.shape[-1]
    micros = table.shape[0] // cores
    small = [(2 * depth, micros, 1, width)] + [(depth, micros, 1, width)] * 3
    small += [(depth, width), (depth, width), (depth, 3, width), (depth, width), (depth, width)]
    small += [(depth, width), (depth, width), (depth, 2, width)]

    def whole(shape):
        return pl.BlockSpec(shape, lambda i: (0,) * len(shape))

    got = pl.pallas_call(
        partial(finish_kernel, cores, depth),
        grid=(steps,),
        out_shape=[struct(*value.shape) for value in wide] + [struct(*shape) for shape in small],
        in_specs=[whole(table.shape)] + blocks,
        out_specs=blocks + [whole(shape) for shape in small],
        compiler_params=pltpu.CompilerParams(vmem_limit_bytes=60 * 1024 * 1024),
    )(table, *wide)
    shares = [value.reshape(whole.shape) for value, whole in zip(got, (out_share, back_share))]
    entry, leave, key, content, gate = [
        value.reshape(whole.shape) for value, whole in zip(got[2:7], sums)
    ]
    small = got[7:]
    return (*shares, *small[:9], entry, leave, *small[9:], key, content, gate)


def run_plain(
    residual_entering,
    upstream_sensitivity,
    piece_lead_lines,
    dividend_start,
    divisor_start,
    power_offset_start,
    attend_standard_scale,
    attend_standard_offset,
    attend_lag_fractions,
    fading_log_rate,
    reward_first_word,
    attend_entry_matrix,
    attend_exit_matrix,
    feed_standard_scale,
    feed_standard_offset,
    feed_lag_fractions,
    feed_lookup_matrix,
    feed_content_matrix,
    feed_gate_matrix,
):
    sections = lax.axis_size("section")
    micro = lax.axis_index("section")
    length, share = residual_entering.shape[2:]
    depth = attend_entry_matrix.shape[0]

    def own(array):
        return lax.dynamic_index_in_dim(array, micro, 0, keepdims=False)

    blank = jnp.zeros((1, share), jnp.float32)
    lead = lax.dynamic_index_in_dim(piece_lead_lines[:, :, 0], micro, 1, keepdims=False)
    starts = [
        lax.dynamic_index_in_dim(start[:, :, 0], micro, 1, keepdims=False)
        for start in (dividend_start, divisor_start, power_offset_start)
    ]
    small_rows, wkv_rows = [], []
    for level in range(depth):
        for gain, bias, mix, j in (
            (attend_standard_scale, attend_standard_offset, attend_lag_fractions, 2 * level),
            (feed_standard_scale, feed_standard_offset, feed_lag_fractions, 2 * level + 1),
        ):
            rows = [gain[level][None], bias[level][None], lead[j][None], mix[level]]
            rows += [blank] * (5 - mix.shape[1])
            small_rows.append(jnp.concatenate(rows, axis=0))
        wkv_rows.append(
            jnp.stack(
                [fading_log_rate[level], reward_first_word[level]]
                + [start[level] for start in starts]
                + [blank[0]] * 3
            )
        )
    small_own = jnp.stack(small_rows)
    small_full = lax.all_gather(small_own, "tp", axis=2, tiled=True)

    rows = own(residual_entering)[0]
    kept = []
    for level in range(depth):
        for j in (2 * level, 2 * level + 1):
            if j % 2 == 0:
                rows, saved = time_forward_plain(
                    rows, small_full[j], small_own[j], wkv_rows[level],
                    attend_entry_matrix[level], attend_exit_matrix[level],
                )
            else:
                rows, saved = channel_forward_plain(
                    rows, small_full[j], small_own[j],
                    feed_lookup_matrix[level], feed_content_matrix[level], feed_gate_matrix[level],
                )
            kept.append(saved)

    def to_tokens(value):
        pieces = value.reshape(sections, length // sections, share)
        return lax.all_to_all(pieces, "section", 0, 0)[:, None]

    out_share = to_tokens(rows)
    grad = own(upstream_sensitivity)[0]
    small_grads, wkv_grads = [None] * (2 * depth), [None] * depth
    weight_grads = [None] * (2 * depth)
    summed = None
    for level in reversed(range(depth)):
        for j in (2 * level + 1, 2 * level):
            if j % 2 == 0:
                grad, small_grads[j], wkv_grads[level], weights = time_backward_plain(
                    grad, kept[j], small_full[j], small_own[j], wkv_rows[level],
                    attend_entry_matrix[level], attend_exit_matrix[level],
                )
            else:
                grad, small_grads[j], weights = channel_backward_plain(
                    grad, kept[j], small_full[j], small_own[j],
                    feed_lookup_matrix[level], feed_content_matrix[level], feed_gate_matrix[level],
                )
            weight_grads[j] = weights
        both = weight_grads[2 * level + 1], weight_grads[2 * level]
        if summed is not None:
            both, summed = lax.optimization_barrier((both, summed))
            weight_grads[2 * level + 3], weight_grads[2 * level + 2] = summed
        summed = lax.psum(both, ("section", "seq"))
    weight_grads[1], weight_grads[0] = summed
    back_share = to_tokens(grad)

    table = jnp.stack(small_grads + wkv_grads)
    tables = lax.all_gather(table, ("section", "seq"), axis=0)
    sums = [
        jnp.stack([weight_grads[2 * level + kind][place] for level in range(depth)])
        for kind, place in ((0, 0), (0, 1), (1, 0), (1, 1), (1, 2))
    ]
    return out_share, back_share, tables, sums


def per_device(*arrays):
    residual_entering, lookup = arrays[0], arrays[16]
    sections, cores = lax.axis_size("section"), lax.axis_size("seq")
    micros, unused, length, share = residual_entering.shape
    depth, features, hidden = lookup.shape
    fits = sections == 4 and cores == 2 and micros == sections and length == sections * CHUNK
    fits = fits and share % 256 == 0 and features % 256 == 0 and hidden % 256 == 0 and hidden % share == 0
    fits = fits and 2 < lax.axis_size("tp") <= LANES // SUB
    if fits:
        return run_fast(*arrays)
    out_share, back_share, table, sums = run_plain(*arrays)
    tables = table.reshape(sections, cores, *table.shape[1:])
    mine = lax.dynamic_index_in_dim(tables, lax.axis_index("seq"), 1, keepdims=False)
    total = jnp.sum(tables, axis=(0, 1))
    prev_grad = jnp.moveaxis(mine[:, : 2 * depth, 2], 0, 1)[:, :, None]
    state_grads = [jnp.moveaxis(mine[:, 2 * depth :, 2 + i], 0, 1)[:, :, None] for i in range(3)]

    weights = [grad.astype(jnp.float32) for grad in sums]
    return (
        out_share,
        back_share,
        prev_grad,
        *state_grads,
        total[0 : 2 * depth : 2, 0],
        total[0 : 2 * depth : 2, 1],
        total[0 : 2 * depth : 2, 3:6],
        total[2 * depth :, 0],
        total[2 * depth :, 1],
        weights[0],
        weights[1],
        total[1 : 2 * depth : 2, 0],
        total[1 : 2 * depth : 2, 1],
        total[1 : 2 * depth : 2, 3:5],
        weights[2],
        weights[3],
        weights[4],
    )


def solution(mesh):
    rows = P(None, "seq", None, "tp")
    line, mix = P(None, "tp"), P(None, None, "tp")
    columns, depths = P(None, None, "tp"), P(None, "tp", None)
    entry = P(None, None, None, "tp")
    state = P(None, None, "seq", "tp")
    tokens = P(None, "seq", "section", "tp")
    return jax.shard_map(
        per_device,
        mesh=mesh,
        in_specs=(
            rows, rows, state, state, state, state,
            line, line, mix, line, line, entry, depths,
            line, line, mix, columns, depths, columns,
        ),
        out_specs=(
            tokens, tokens, state, state, state, state,
            line, line, mix, line, line, entry, depths,
            line, line, mix, columns, depths, columns,
        ),
        check_vma=False,
    )
```

time: 5400 us -> 330 us (0.06)
  other arithmetic: 2830 us -> 0 us
  waiting for transfers between devices: 1520 us -> 0 us
  local copies, waits for them, and re-layouts: 433 us -> 2.59 us
  Pallas kernels: 0 us -> 325 us
  blocking collectives: 297 us -> 0 us
  matrix products: 157 us -> 0 us
  starting transfers between devices: 108 us -> 0 us
    reduce_sum x325 -> x0, other arithmetic: 1430 us -> none  [the longest x84 705 us: advance(): jnp.sum(weights * value_block[None, :, :], axis=1)]
    all_gather x21 -> x0, waiting for transfers between devices: 725 us -> none  [the longest x14 592 us: spread(): lax.all_gather(normed_share, 'tp', axis=1, tiled=True)]
    reduce_max x140 -> x0, other arithmetic: 670 us -> none  [the longest x84 614 us: advance(): jnp.max(spread_exp, axis=1)]
    reduce_scatter x16 -> x0, waiting for transfers between devices: 421 us -> none  [the longest x7 251 us: per_device(): lax.psum_scatter(branch_rows, 'tp', scatter_dimension=1, tiled=True)]
    pallas_call x0 -> x2, Pallas kernels: none -> 325 us  [the longest x1 309 us: run_kernel(): pl.pallas_call(body, out_shape=[out for out, inside in outs], in_specs=[s...]
    psum x1 -> x0, waiting for transfers between devices: 256 us -> none  [per_device(): lax.psum((grad_tm_gain, grad_tm_bias, grad_tm_mix, grad_decay, reward_der...]
    scatter-add x74 -> x0, other arithmetic: 200 us -> none  [the longest x7 51 us: per_device(): grad_cm_key.at[picked_level].add(channel_scale * channel_part[0])]
    psum x16 -> x0, blocking collectives: 166 us -> none  [the longest x7 63.9 us: per_device(): total_first, total_second = lax.psum((first_sum, second_sum), 'tp')]
  transfers between devices with their start and end apart: 57 -> 0, of which waited for: 47 -> 0; matrix products, arithmetic and copies ran while one was open for 13% -> 0% of each run, Pallas kernels for 0% -> 0%
where the time goes in v1:
time: 330 us; the launch traced here: 329 us
  Pallas kernels  325 us (98%)
    pallas_call x1, Pallas kernels, run_kernel(): pl.pallas_call(body, out_shape=[out for out, inside in outs], in_specs=[s...  309 us
    pallas_call x1, Pallas kernels, finish(): pl.pallas_call(partial(finish_kernel, cores, depth), grid=(steps,), out_s...  16.8 us

profile of v1, /device:TPU:9, one launch (start us, length us, event | category | flops | bytes accessed | tf_op | source)
XLA Modules:
  0.0 328.7 jit_solution(12772309070185808999)
XLA Ops:
  0.7 1.3 copy.38.attend_mix
  1.9 308.7 %shard_map.330 = (f32[4,1,128,256]{3,2,1,0:T(8,128)}, f32[4,1,128,256]{3,2,1,0:T(8,128)}, f32[8,6,8,256]{3,2,1,0:T(8,128)}, bf16[2,3,1024,256]{3,2,1,0:T(8,128)(...) custom-call(f32[4,1,512,256]{3,2,1,0:T(8,128)} %rows_hbm.1, ...), custom_call_target="tpu_custom_call" | custom-call | flops 20937965568 | bytes 33554432 | tf_op jit(solution)/shard_map/pallas_call | solution.py:1317
  310.7 16.8 %shard_map.331 = (f32[512,256]{1,0:T(8,128)}, f32[512,256]{1,0:T(8,128)}, f32[6144,256]{1,0:T(8,128)}, f32[512,1024]{1,0:T(8,128)}, f32[2048,1024]{1,0:T(8,128)}...) custom-call(f32[8,6,8,256]{3,2,1,0:T(8,128)} %get-tuple-element.46.t, ...), custom_call_target="tpu_custom_call" | custom-call | tf_op jit(solution)/shard_map/pallas_call | solution.py:1440
  327.4 1.3 copy.41

commit v2 on v1

--- a/solution.py
+++ b/solution.py
@@ -198,6 +198,7 @@
 CHUNK = 128
 LANES = 128
 SUB = 8
+PAIR = 2
 MESH = pl.DeviceIdType.MESH
 NO_POWER = -1e30
 
@@ -207,12 +208,12 @@
     wide = jnp.zeros((CHUNK, LANES), jnp.float32)
     for place, column in enumerate(columns):
         wide = jnp.where(lane == place, column, wide)
-    return jnp.transpose(wide)[:SUB]
+    return jnp.transpose(wide)[:PAIR]
 
 
 def to_columns(tiles):
     count = len(tiles)
-    filler = [jnp.zeros((LANES - SUB * count, CHUNK), jnp.float32)]
+    filler = [jnp.zeros((LANES - PAIR * count, CHUNK), jnp.float32)]
     return jnp.transpose(jnp.concatenate(list(tiles) + filler, axis=0))
 
 
@@ -481,9 +482,9 @@
     count, width = peers.count, peers.width
     tiles.arrived(c)
     columns = to_columns([tiles.stat[source, c] for source in range(count)])
-    middles = [columns[:, SUB * source : SUB * source + 1] for source in range(count)]
+    middles = [columns[:, PAIR * source : PAIR * source + 1] for source in range(count)]
     center = sum(middles) / count
-    square = sum(columns[:, SUB * source + 1 : SUB * source + 2] for source in range(count))
+    square = sum(columns[:, PAIR * source + 1 : PAIR * source + 2] for source in range(count))
     square = square + width * sum((middle - center) * (middle - center) for middle in middles)
     inv_std = lax.rsqrt(square / (count * width) + epsilon)
     std_ref[rows_of(c), :] = jnp.broadcast_to(inv_std, (CHUNK, LANES))
@@ -692,26 +693,23 @@
 
 
 STEPS = 7
-COPIES = 21
+COPIES = 15
+EVERY = slice(None)
 
 
 class Summed:
     def __init__(self, grad, core_land, cross_land, own_land, result, sems):
         self.grad, self.core_land, self.cross_land, self.own_land = grad, core_land, cross_land, own_land
         self.result, self.sems = result, sems
-        self.rows = grad.shape[-2]
-        self.half, self.piece, self.sub = self.rows // 2, self.rows // 8, self.rows // 16
-        self.q, self.s = lax.axis_index("seq"), lax.axis_index("section")
-        self.y, self.x = lax.div(self.s, 2), lax.rem(self.s, 2)
+        self.lead = (EVERY,) * (len(grad.shape) - 6)
+        self.q, section = lax.axis_index("seq"), lax.axis_index("section")
+        self.y, self.x = lax.div(section, 2), lax.rem(section, 2)
         self.sibling = {"seq": 1 - self.q}
-        self.over_x = {"section": self.s + 1 - 2 * self.x}
-        self.over_y = {"section": self.s + 2 - 4 * self.y}
-
-    def at(self, ref, start, size):
-        return ref.at[pl.ds(pl.multiple_of(start, 16), size), :]
-
-    def spot(self, q, y, x, part):
-        return q * self.half + (2 * y + x) * self.piece + part * self.sub
+        self.over_x = {"section": section + 1 - 2 * self.x}
+        self.over_y = {"section": section + 2 - 4 * self.y}
+
+    def at(self, ref, *place):
+        return ref.at[(*self.lead, *place)]
 
     def send(self, which, source, target, place):
         return pltpu.make_async_remote_copy(
@@ -719,134 +717,114 @@
             device_id=place, device_id_type=MESH,
         )
 
-    def add(self, start, land, land_start, size):
-        columns = self.grad.shape[-1]
-        block = min(size, max(16, 32768 // columns))
-
+    def share(self, which, held, device, *place):
+        return self.send(which, self.at(held, *place), self.at(self.result, *place), device)
+
+    def arrive(self, which, ref, *place):
+        view = self.at(ref, *place)
+        self.send(which, view, view, self.sibling).wait_recv()
+
+    def add(self, place, land, land_place):
+        mine, come = self.at(self.grad, *place), self.at(land, *land_place)
+        rows = mine.shape[-2]
+        block = min(rows, 32)
+        for k in range(3 if self.lead else 1):
+            for start in range(0, rows, block):
+                view = (*((k,) if self.lead else ()), slice(start, start + block), EVERY)
+                mine[view] = (mine[view].astype(jnp.float32) + come[view].astype(jnp.float32)).astype(jnp.bfloat16)
+
+    def add_half(self):
         def step(i, unused):
-            mine = self.at(self.grad, start + i * block, block)
-            come = self.at(land, land_start + i * block, block)
-            mine[...] = (mine[...].astype(jnp.float32) + come[...].astype(jnp.float32)).astype(jnp.bfloat16)
+            place = lax.div(i, 4), lax.rem(lax.div(i, 2), 2), lax.rem(i, 2)
+            self.add((self.q, *place), self.core_land, place)
             return unused
 
-        lax.fori_loop(0, size // block, step, 0)
+        lax.fori_loop(0, 8, step, 0)
 
     def to_core(self):
-        other = self.at(self.grad, (1 - self.q) * self.half, self.half)
-        return [self.send(0, other, self.core_land, self.sibling)]
-
-    def cross(self, y, x):
-        out = []
-        for k in (0, 1):
-            for part, place, (py, px) in (
-                (0, self.over_x, (k, 1 - x)), (1, self.over_y, (1 - y, k)),
-            ):
-                spot = self.spot(0, py, px, part)
-                out.append(
-                    self.send(
-                        1 + 2 * k + part, self.at(self.grad, self.q * self.half + spot, self.sub),
-                        self.at(self.cross_land, spot, self.sub), place,
-                    )
-                )
-        return out
+        return [self.send(0, self.at(self.grad, 1 - self.q), self.core_land, self.sibling)]
+
+    def cross(self):
+        first, second = (EVERY, 1 - self.x, 0), (1 - self.y, EVERY, 1)
+        return [
+            self.send(1, self.at(self.grad, self.q, *first), self.at(self.cross_land, *first), self.over_x),
+            self.send(2, self.at(self.grad, self.q, *second), self.at(self.cross_land, *second), self.over_y),
+        ]
 
     def own(self):
-        out = []
-        for part, place, (py, px) in (
-            (0, self.over_y, (1 - self.y, self.x)), (1, self.over_x, (self.y, 1 - self.x)),
-        ):
-            source = self.at(self.grad, self.spot(self.q, py, px, part), self.sub)
-            out.append(self.send(5 + part, source, self.at(self.own_land, part * self.sub, self.sub), place))
-        return out
-
-    def share(self, which, q, y, x, part, size, place, held):
-        spot = self.spot(q, y, x, part)
-        return self.send(which, self.at(held, spot, size), self.at(self.result, spot, size), place)
-
-    def back_own(self, q, y, x):
+        q, y, x = self.q, self.y, self.x
         return [
-            self.share(7, q, y, x, 0, self.sub, self.over_y, self.grad),
-            self.share(8, q, y, x, 1, self.sub, self.over_x, self.grad),
-            self.share(9, q, y, x, 0, self.piece, self.sibling, self.grad),
+            self.send(3, self.at(self.grad, q, 1 - y, x, 0), self.at(self.own_land, 0), self.over_y),
+            self.send(4, self.at(self.grad, q, y, 1 - x, 1), self.at(self.own_land, 1), self.over_x),
+        ]
+
+    def back_own(self):
+        q, y, x = self.q, self.y, self.x
+        return [
+            self.share(5, self.grad, self.over_y, q, y, x, 0), self.share(6, self.grad, self.over_x, q, y, x, 1),
+            self.share(7, self.grad, self.sibling, q, y, x),
         ]
 
     def back_cross(self):
         q, y, x = self.q, self.y, self.x
         return [
-            self.share(10, q, y, x, 0, self.sub, self.over_x, self.result),
-            self.share(11, q, 1 - y, x, 0, self.sub, self.over_x, self.result),
-            self.share(12, q, y, x, 1, self.sub, self.over_y, self.result),
-            self.share(13, q, y, 1 - x, 1, self.sub, self.over_y, self.result),
-            self.share(14, q, 1 - y, x, 0, self.sub, self.sibling, self.result),
-            self.share(15, q, y, 1 - x, 1, self.sub, self.sibling, self.result),
+            self.share(8, self.result, self.over_x, q, EVERY, x, 0), self.share(9, self.result, self.over_y, q, y, EVERY, 1),
+            self.share(10, self.result, self.sibling, q, 1 - y, x, 0),
+            self.share(11, self.result, self.sibling, q, y, 1 - x, 1),
         ]
 
     def back_core(self):
         q, y, x = self.q, self.y, self.x
         return [
-            self.share(16, q, y, 1 - x, 0, self.sub, self.sibling, self.result),
-            self.share(17, q, 1 - y, 1 - x, 0, self.sub, self.sibling, self.result),
-            self.share(18, q, 1 - y, x, 1, self.sub, self.sibling, self.result),
-            self.share(19, q, 1 - y, 1 - x, 1, self.sub, self.sibling, self.result),
+            self.share(12, self.result, self.sibling, q, EVERY, 1 - x, 0),
+            self.share(13, self.result, self.sibling, q, 1 - y, EVERY, 1),
         ]
 
     def keep(self):
-        spot = self.spot(self.q, self.y, self.x, 0)
-        return pltpu.make_async_copy(
-            self.at(self.grad, spot, self.piece), self.at(self.result, spot, self.piece), self.sems[0].at[20]
-        )
-
-    def arrive(self, which, ref, start, size):
-        view = self.at(ref, start, size)
-        self.send(which, view, view, self.sibling).wait_recv()
+        place = self.q, self.y, self.x
+        return pltpu.make_async_copy(self.at(self.grad, *place), self.at(self.result, *place), self.sems[0].at[14])
 
     def step(self, number):
         q, y, x = self.q, self.y, self.x
+        started = []
         if number == 0:
             started = self.to_core()
         elif number == 1:
-            self.arrive(0, self.core_land, 0, self.half)
-            self.add(q * self.half, self.core_land, 0, self.half)
-            started = self.cross(y, x)
+            self.arrive(0, self.core_land)
+            self.add_half()
+            started = self.cross()
         elif number == 2:
+            self.arrive(1, self.cross_land, EVERY, x, 0)
+            self.arrive(2, self.cross_land, y, EVERY, 1)
             for k in (0, 1):
-                for part, (py, px) in ((0, (k, x)), (1, (y, k))):
-                    spot = self.spot(0, py, px, part)
-                    self.arrive(1 + 2 * k + part, self.cross_land, spot, self.sub)
-                    self.add(q * self.half + spot, self.cross_land, spot, self.sub)
+                self.add((q, k, x, 0), self.cross_land, (k, x, 0))
+                self.add((q, y, k, 1), self.cross_land, (y, k, 1))
             started = self.own()
         elif number == 3:
             for part in (0, 1):
-                self.arrive(5 + part, self.own_land, part * self.sub, self.sub)
-                self.add(self.spot(q, y, x, part), self.own_land, part * self.sub, self.sub)
-            started = self.back_own(q, y, x) + [self.keep()]
+                self.arrive(3 + part, self.own_land, part)
+                self.add((q, y, x, part), self.own_land, (part,))
+            started = self.back_own() + [self.keep()]
         elif number == 4:
-            self.arrive(7, self.result, self.spot(q, 1 - y, x, 0), self.sub)
-            self.arrive(8, self.result, self.spot(q, y, 1 - x, 1), self.sub)
+            self.arrive(5, self.result, q, 1 - y, x, 0)
+            self.arrive(6, self.result, q, y, 1 - x, 1)
             self.keep().wait()
             started = self.back_cross()
         elif number == 5:
-            self.arrive(9, self.result, self.spot(1 - q, y, x, 0), self.piece)
-            self.arrive(10, self.result, self.spot(q, y, 1 - x, 0), self.sub)
-            self.arrive(11, self.result, self.spot(q, 1 - y, 1 - x, 0), self.sub)
-            self.arrive(12, self.result, self.spot(q, 1 - y, x, 1), self.sub)
-            self.arrive(13, self.result, self.spot(q, 1 - y, 1 - x, 1), self.sub)
+            self.arrive(7, self.result, 1 - q, y, x)
+            self.arrive(8, self.result, q, EVERY, 1 - x, 0)
+            self.arrive(9, self.result, q, 1 - y, EVERY, 1)
             started = self.back_core()
         else:
-            o = 1 - q
-            self.arrive(14, self.result, self.spot(o, 1 - y, x, 0), self.sub)
-            self.arrive(15, self.result, self.spot(o, y, 1 - x, 1), self.sub)
-            self.arrive(16, self.result, self.spot(o, y, 1 - x, 0), self.sub)
-            self.arrive(17, self.result, self.spot(o, 1 - y, 1 - x, 0), self.sub)
-            self.arrive(18, self.result, self.spot(o, 1 - y, x, 1), self.sub)
-            self.arrive(19, self.result, self.spot(o, 1 - y, 1 - x, 1), self.sub)
-            started = []
+            self.arrive(10, self.result, 1 - q, 1 - y, x, 0)
+            self.arrive(11, self.result, 1 - q, y, 1 - x, 1)
+            self.arrive(12, self.result, 1 - q, EVERY, 1 - x, 0)
+            self.arrive(13, self.result, 1 - q, 1 - y, EVERY, 1)
         for copy in started:
             copy.start()
 
     def sent_grad(self):
-        copies = self.to_core() + self.cross(self.y, self.x) + self.own() + self.back_own(self.q, self.y, self.x)
-        for copy in copies:
+        for copy in self.to_core() + self.cross() + self.own() + self.back_own():
             copy.wait_send()
 
     def sent_rest(self):
@@ -857,7 +835,7 @@
 GROUPS = (
     (0, (1,), (1, 2, 4, 5, 6, 11)),
     (0, (0, 2), (0, 1, 3, 4, 5, 11)),
-    (1, (3, 4, 5, 6), (1, 2, 4, 5, 6, 12)),
+    (1, (3, 4), (1, 2, 4, 5, 6, 12)),
 )
 
 
@@ -905,7 +883,8 @@
         full_ref[j, 0:1, mine] = gain[level : level + 1, :]
         full_ref[j, 1:2, mine] = bias[level : level + 1, :]
         full_ref[j, 2:3, mine] = lead_ref[j, micro]
-        full_ref[j, 3 : 3 + mix.shape[1], mine] = mix[level]
+        for i in range(mix.shape[0] if j % 2 == 0 else mix.shape[1]):
+            full_ref[j, 3 + i : 4 + i, mine] = mix[i, level : level + 1] if j % 2 == 0 else mix[level, i : i + 1]
     gather = Gather(peers, pay, (gs, gr))
     tiles = Tiles(peers, stat, (ts, tr))
     scatter = Scatter(peers, part, stage, land, (ss, sr))
@@ -923,10 +902,7 @@
             (gate_grad, gate_core, gate_cross, gate_own, gate_sum),
         )
         entry = (entry_grad, entry_core, entry_cross, entry_own, entry_sum)
-        parts += tuple(
-            (*(ref.at[i] for ref in entry[:4]), entry_sum.at[:, i]) for i in range(3)
-        )
-        parts += ((exit_grad, exit_core, exit_cross, exit_own, exit_sum),)
+        parts += (entry, (exit_grad, exit_core, exit_cross, exit_own, exit_sum))
         out = []
         for place in GROUPS[group][1]:
             grad, core_land, cross_land, own_land, result = parts[place]
@@ -1040,18 +1016,22 @@
         def _():
             last_ref[0:1, :] = full_ref[j, 2:3, :]
 
-        mix_chunk(
-            peers, c, pay.at[lax.rem(j, 2)], tiles, full_ref.at[j], mixed_ref.at[:, pl.ds(0, CHUNK)], normal_ref.at[j], edge_ref.at[j], std_ref.at[j],
-            last_ref,
-        )
+        def mix(count_mixed):
+            mix_chunk(
+                peers, c, pay.at[lax.rem(j, 2)], tiles, full_ref.at[j], mixed_ref.at[pl.ds(0, count_mixed), pl.ds(0, CHUNK)],
+                normal_ref.at[j], edge_ref.at[j], std_ref.at[j], last_ref,
+            )
+
         level = lax.div(j, 2)
 
         @pl.when(lax.rem(j, 2) == 0)
         def _():
+            mix(3)
             attend_forward(level, c)
 
         @pl.when(lax.rem(j, 2) == 1)
         def _():
+            mix(2)
             feed_forward(level, c)
 
         gather.sent(c, j)
@@ -1202,21 +1182,30 @@
                 copy.start()
 
     def weigh(place, level):
-        for source in range(count):
-            block = peers.columns(source)
+        if place == 4:
+            for source in range(count):
+                block = peers.columns(source)
+                grad = inner_rows(output_ref[...], pay[1, :, block]).astype(jnp.bfloat16)
+                exit_grad[..., block] = grad.reshape(*exit_grad.shape[:-1], width)
+            return
+        for i in range(4):
+            at = i // 2, i % 2
+            if place == 1:
+                rows = hidden_width // 4
+                grad = inner_rows(hidden_ref[level, :, i * rows : (i + 1) * rows], pay[0]).astype(jnp.bfloat16)
+                content_grad[at] = grad.reshape(content_grad.shape[2:])
+                continue
+            rows = slice(i * (pay.shape[2] // 4), (i + 1) * (pay.shape[2] // 4))
             if place == 0:
-                key_grad[block, :] = inner_rows(mixed_ref[0, :, block], hidden_grad[...]).astype(jnp.bfloat16)
+                grad = inner_rows(mixed_ref[0, :, rows], hidden_grad[...]).astype(jnp.bfloat16)
+                key_grad[at] = grad.reshape(key_grad.shape[2:])
             elif place == 2:
-                gate_grad[block, :] = inner_rows(mixed_ref[1, :, block], pre_grads[0]).astype(jnp.bfloat16)
-            elif 3 <= place < 6:
-                i = place - 3
-                entry_grad[i, block, :] = inner_rows(mixed_ref[i, :, block], pre_grads[i]).astype(jnp.bfloat16)
-            elif place == 6:
-                exit_grad[:, block] = inner_rows(output_ref[...], pay[1, :, block]).astype(jnp.bfloat16)
-        if place == 1:
-            for start in range(0, hidden_width, width):
-                block = slice(start, start + width)
-                content_grad[block, :] = inner_rows(hidden_ref[level, :, block], pay[0]).astype(jnp.bfloat16)
+                grad = inner_rows(mixed_ref[1, :, rows], pre_grads[0]).astype(jnp.bfloat16)
+                gate_grad[at] = grad.reshape(gate_grad.shape[2:])
+            else:
+                for k in range(3):
+                    grad = inner_rows(mixed_ref[k, :, rows], pre_grads[k]).astype(jnp.bfloat16)
+                    entry_grad[(k, *at)] = grad.reshape(entry_grad.shape[3:])
 
     base, final = chunks + count - 1, passes * period + chunks - 1
 
@@ -1352,18 +1341,22 @@
     def held(*shape, dtype=F32):
         return pltpu.VMEM(shape, dtype)
 
-    def rows_cut(by):
-        return [held(*shape[:-2], shape[-2] // by, shape[-1], dtype=BF16) for shape in shapes]
+    def cut(*parts):
+        return [(*shape[:-2], *parts, shape[-2] // 16, shape[-1]) for shape in shapes]
 
     outs = [(shares, False), (shares, False), (struct(sections * cores, subs + depth, SUB, width), True)]
-    outs += [(struct(*weight.shape, dtype=BF16), False) for weight in weights]
+    outs += [(struct(depth, *shape, dtype=BF16), False) for shape in cut(2, 2, 2, 2)]
     scratch = [held(subs, length, features, dtype=BF16), held(subs, length, LANES), held(*lines), held(*lines)]
     scratch += [held(*lines), held(depth, 3, *lines[1:]), held(*lines)]
     scratch += [held(depth, length, hidden, dtype=BF16)] * 2 + [held(*lines)] * 2
     scratch += [held(subs, SUB, features)] * 2 + [held(length, width), held(groups, length, LANES)] * 2
-    scratch += [held(*weight.shape, dtype=BF16) for weight in weights] + rows_cut(1) + rows_cut(2) + rows_cut(2) + rows_cut(8)
+    scratch += [held(*weight.shape, dtype=BF16) for weight in weights]
     scratch += [
-        held(2, length, features, dtype=BF16), held(count, chunks, SUB, LANES), held(length, features),
+        held(*shape, dtype=BF16)
+        for shape in cut(2, 2, 2, 2) + cut(2, 2, 2) + cut(2, 2, 2) + cut(2)
+    ]
+    scratch += [
+        held(2, length, features, dtype=BF16), held(count, chunks, PAIR, LANES), held(length, features),
         held(length, features, dtype=BF16), held(2, length, features + width, dtype=BF16),
     ]
     scratch += [
@@ -1375,13 +1368,14 @@
     scratch += [pltpu.SemaphoreType.DMA((n,)) for n in (len(weights), groups, groups)] + pair_of((count - 1,))
     scratch += pair_of((sections, groups)) + pair_of((sections, groups))
     scratch += pair_of((2, 2, count - 1, chunks)) + pair_of((count - 1, chunks)) + pair_of((2, 2, count, chunks))
-    scratch += pair_of((subs, count - 1)) + pair_of((depth, len(weights) + 2, COPIES))
+    scratch += pair_of((subs, count - 1)) + pair_of((depth, len(weights), COPIES))
     scratch += pair_of((sections * cores - 1,))
     operands = [(residual_entering, False), (upstream_sensitivity, False)]
     operands += [
         (value, True)
         for value in (
-            piece_lead_lines, *starts, attend_standard_scale, attend_standard_offset, attend_lag_fractions,
+            piece_lead_lines, *starts, attend_standard_scale, attend_standard_offset,
+            jnp.swapaxes(attend_lag_fractions, 0, 1),
             fading_log_rate, reward_first_word, feed_standard_scale, feed_standard_offset, feed_lag_fractions,
         )
     ]
@@ -1389,7 +1383,7 @@
     out_share, back_share, table, *sums = run_kernel(
         partial(both_kernel, count, sections, cores, depth), 0, outs, scratch, operands, 3 * flops
     )
-    return finish(cores, depth, out_share, back_share, table, sums)
+    return finish(cores, depth, out_share, back_share, table, sums, [weight.shape for weight in weights])
 
 
 def finish_kernel(cores, depth, table_ref, *refs):
@@ -1416,14 +1410,16 @@
                 total = sum(table_ref[place, j] for place in range(places))
                 gain[level : level + 1, :] = total[0:1]
                 bias[level : level + 1, :] = total[1:2]
-                mix[level] = total[3 : 3 + mix.shape[1]]
+                for i in range(mix.shape[0] if mix is attend_mix else mix.shape[1]):
+                    place = (i, slice(level, level + 1)) if mix is attend_mix else (level, slice(i, i + 1))
+                    mix[place] = total[3 + i : 4 + i]
             total = sum(table_ref[place, subs + level] for place in range(places))
             decay[level : level + 1, :] = total[0:1]
             bonus[level : level + 1, :] = total[1:2]
 
 
-def finish(cores, depth, out_share, back_share, table, sums):
-    steps = 8
+def finish(cores, depth, out_share, back_share, table, sums, shapes):
+    steps = 4
     wide = [value.reshape(-1, value.shape[-1]) for value in (out_share, back_share, *sums)]
     blocks = [
         pl.BlockSpec((value.shape[0] // steps, value.shape[1]), lambda i: (i, 0)) for value in wide
@@ -1431,7 +1427,7 @@
     width = table.shape[-1]
     micros = table.shape[0] // cores
     small = [(2 * depth, micros, 1, width)] + [(depth, micros, 1, width)] * 3
-    small += [(depth, width), (depth, width), (depth, 3, width), (depth, width), (depth, width)]
+    small += [(depth, width), (depth, width), (3, depth, width), (depth, width), (depth, width)]
     small += [(depth, width), (depth, width), (depth, 2, width)]
 
     def whole(shape):
@@ -1447,9 +1443,10 @@
     )(table, *wide)
     shares = [value.reshape(whole.shape) for value, whole in zip(got, (out_share, back_share))]
     entry, leave, key, content, gate = [
-        value.reshape(whole.shape) for value, whole in zip(got[2:7], sums)
+        value.reshape(shape) for value, shape in zip(got[2:7], shapes)
     ]
-    small = got[7:]
+    small = list(got[7:])
+    small[6] = jnp.swapaxes(small[6], 0, 1)
     return (*shares, *small[:9], entry, leave, *small[9:], key, content, gate)
 
 

time: 330 us -> 319 us (0.967)
  Pallas kernels: 325 us -> 318 us
    pallas_call x1, Pallas kernels: 309 us -> 303 us  [run_kernel(): pl.pallas_call(body, out_shape=[out for out, inside in outs], in_specs=[s...]
where the time goes in v2:
time: 319 us
  Pallas kernels  318 us (100%)
    pallas_call x1, Pallas kernels, run_kernel(): pl.pallas_call(body, out_shape=[out for out, inside in outs], in_specs=[s...  303 us
    pallas_call x1, Pallas kernels, finish(): pl.pallas_call(partial(finish_kernel, cores, depth), grid=(steps,), out_s...  15.2 us

profile of v2, /device:TPU:9, one launch (start us, length us, event | category | flops | bytes accessed | tf_op | source)
XLA Modules:
  0.0 318.8 jit_solution(2663613147158075999)
XLA Ops:
  0.7 302.8 %shard_map.330 = (f32[4,1,128,256]{3,2,1,0:T(8,128)}, f32[4,1,128,256]{3,2,1,0:T(8,128)}, f32[8,6,8,256]{3,2,1,0:T(8,128)}, bf16[2,3,2,2,2,2,64,256]{7,6,5,4,3,2...) custom-call(f32[4,1,512,256]{3,2,1,0:T(8,128)} %rows_hbm.1, ...), custom_call_target="tpu_custom_call" | custom-call | flops 20937965568 | bytes 33554432 | tf_op jit(solution)/shard_map/pallas_call | solution.py:1306
  303.5 15.2 %shard_map.331 = (f32[512,256]{1,0:T(8,128)}, f32[512,256]{1,0:T(8,128)}, f32[6144,256]{1,0:T(8,128)}, f32[512,1024]{1,0:T(8,128)}, f32[2048,1024]{1,0:T(8,128)}...) custom-call(f32[8,6,8,256]{3,2,1,0:T(8,128)} %get-tuple-element.46.t, ...), custom_call_target="tpu_custom_call" | custom-call | tf_op jit(solution)/shard_map/pallas_call | solution.py:1436

commit v3 on v2

--- a/solution.py
+++ b/solution.py
@@ -254,16 +254,40 @@
             ]
 
 
+def halves(value, most):
+    if isinstance(value, int):
+        return value // 2
+    return sum(jnp.where(value >= 2 * k, 1, 0) for k in range(1, most // 2 + 1))
+
+
+def odd(value, most):
+    return value - 2 * halves(value, most)
+
+
+class Here:
+    def __init__(self, names):
+        self.names, self.at = names, {name: lax.axis_index(name) for name in names}
+
+    def device(self, **other):
+        return tuple(other.get(name, self.at[name]) for name in self.names)
+
+
 class Peers:
-    def __init__(self, count, width):
-        self.count, self.width = count, width
-        self.me = lax.axis_index("tp")
+    def __init__(self, here, count, width, passes):
+        self.here, self.count, self.width, self.passes = here, count, width, passes
+        self.me = here.at["tp"]
+        self.others = [lax.rem(self.me + k, count) for k in range(count)]
+        self.sources = [lax.rem(self.me + count - k, count) for k in range(count)]
+        self.beside = jnp.minimum(self.me + 1, count - 1), jnp.maximum(self.me - 1, 0)
 
     def to(self, k):
-        return lax.rem(self.me + k, self.count)
+        return self.others[k]
 
     def source(self, k):
-        return lax.rem(self.me + self.count - k, self.count)
+        return self.sources[k]
+
+    def slot(self, which):
+        return odd(which, self.passes)
 
     def columns(self, owner):
         if isinstance(owner, int):
@@ -272,7 +296,7 @@
 
     def greet(self, others):
         barrier = pltpu.get_barrier_semaphore()
-        places = [{"tp": self.to(k)} for k in range(1, self.count)] + others
+        places = [self.here.device(tp=self.to(k)) for k in range(1, self.count)] + others
         for place in places:
             pl.semaphore_signal(barrier, inc=1, device_id=place, device_id_type=MESH)
         pl.semaphore_wait(barrier, len(places))
@@ -280,7 +304,7 @@
     def copy(self, device, source_ref, target_ref, send, receive):
         return pltpu.make_async_remote_copy(
             src_ref=source_ref, dst_ref=target_ref, send_sem=send, recv_sem=receive,
-            device_id={"tp": device}, device_id_type=MESH,
+            device_id=self.here.device(tp=device), device_id_type=MESH,
         )
 
 
@@ -316,9 +340,9 @@
         self.peers, self.pay, self.sems = peers, pay, sems
 
     def copy(self, way, hop, c, owner, which):
-        slot = lax.rem(which, self.pay.shape[0])
+        slot = self.peers.slot(which)
         block = self.pay.at[slot, rows_of(c), self.peers.columns(owner)]
-        device = jnp.clip(self.peers.me + (1 - 2 * way), 0, self.peers.count - 1)
+        device = self.peers.beside[way]
         return self.peers.copy(
             device, block, block, self.sems[0].at[slot, way, hop - 1, c], self.sems[1].at[slot, way, hop - 1, c]
         )
@@ -367,7 +391,7 @@
         return self.peers.columns(jnp.where(target == owner, self.peers.count, target))
 
     def copy(self, way, c, target, which):
-        slot, device = lax.rem(which, 2), jnp.clip(self.peers.me + (1 - 2 * way), 0, self.peers.count - 1)
+        slot, device = self.peers.slot(which), self.peers.beside[way]
         return self.peers.copy(
             device, self.stage.at[rows_of(c), self.peers.columns(target)],
             self.land.at[slot, rows_of(c), self.landing(way, target, device)],
@@ -375,7 +399,7 @@
         )
 
     def come(self, way, c, target, which):
-        slot, columns = lax.rem(which, 2), self.landing(way, target, self.peers.me)
+        slot, columns = self.peers.slot(which), self.landing(way, target, self.peers.me)
         block = self.land.at[slot, rows_of(c), columns]
         self.peers.copy(
             self.peers.me, block, block, self.sems[0].at[slot, way, target, c], self.sems[1].at[slot, way, target, c]
@@ -435,21 +459,22 @@
     count = peers.count
     period = max(2 * count - 2, chunks + 1)
 
-    def split(at):
-        which, i = lax.div(at, period), lax.rem(at, period)
-        chunk = chunks - 1 - i if backward else i
-        return which, jnp.clip(chunk, 0, chunks - 1), (at >= 0) & (i < chunks) & (which < passes)
-
-    def tick(t):
-        which, c, there = split(t)
-        last = (which == passes) & (lax.rem(t, period) < chunks)
+    def split(w, i, behind):
+        early = i >= behind
+        which, at = jnp.where(early, w, w - 1), jnp.where(early, i - behind, i - behind + period)
+        chunk = chunks - 1 - at if backward else at
+        return which, jnp.clip(chunk, 0, chunks - 1), (which >= 0) & (which < passes) & (at < chunks)
+
+    def tick(w, i):
+        which, c, there = split(w, i, 0)
+        last = (w == passes) & (i < chunks)
 
         @pl.when(there | last)
         def _():
             begin(which, c)
 
         def relay(hop):
-            moved, c_hop, there = split(t - hop)
+            moved, c_hop, there = split(w, i, hop)
 
             @pl.when(there)
             def _():
@@ -458,14 +483,14 @@
         def push(middle):
             for way in (0, 1):
                 lag = scatter.lag(way)
-                moved, c_way, there = split(t - (count - 1) - lag)
+                moved, c_way, there = split(w, i, count - 1 + lag)
 
                 @pl.when(there & ((lag == 1) == middle))
                 def _():
                     scatter.push(way, c_way, moved + before)
 
         relay(count - 1)
-        which, c, there = split(t - (count - 1))
+        which, c, there = split(w, i, count - 1)
 
         @pl.when(there)
         def _():
@@ -618,9 +643,9 @@
     ]
 
 
-def to_sections(sections, rows_ref, tokens_ref, out_hbm, sems):
+def to_sections(here, sections, rows_ref, tokens_ref, out_hbm, sems):
     send, receive = sems
-    micro = lax.axis_index("section")
+    micro = here.at["section"]
     groups = range(tokens_ref.shape[0])
 
     def ends(c, source, g):
@@ -630,7 +655,7 @@
         held, target = ends(c, source, g)
         return pltpu.make_async_remote_copy(
             src_ref=held, dst_ref=target, send_sem=send.at[c, g], recv_sem=receive.at[source, g],
-            device_id={"section": c}, device_id_type=MESH,
+            device_id=here.device(section=c), device_id_type=MESH,
         )
 
     def own(g):
@@ -698,15 +723,11 @@
 
 
 class Summed:
-    def __init__(self, grad, core_land, cross_land, own_land, result, sems):
+    def __init__(self, around, grad, core_land, cross_land, own_land, result, sems):
         self.grad, self.core_land, self.cross_land, self.own_land = grad, core_land, cross_land, own_land
         self.result, self.sems = result, sems
         self.lead = (EVERY,) * (len(grad.shape) - 6)
-        self.q, section = lax.axis_index("seq"), lax.axis_index("section")
-        self.y, self.x = lax.div(section, 2), lax.rem(section, 2)
-        self.sibling = {"seq": 1 - self.q}
-        self.over_x = {"section": section + 1 - 2 * self.x}
-        self.over_y = {"section": section + 2 - 4 * self.y}
+        (self.q, self.y, self.x), (self.sibling, self.over_x, self.over_y) = around
 
     def at(self, ref, *place):
         return ref.at[(*self.lead, *place)]
@@ -735,7 +756,8 @@
 
     def add_half(self):
         def step(i, unused):
-            place = lax.div(i, 4), lax.rem(lax.div(i, 2), 2), lax.rem(i, 2)
+            y, rest = halves(halves(i, 7), 3), i - 4 * halves(halves(i, 7), 3)
+            place = y, halves(rest, 3), odd(rest, 3)
             self.add((self.q, *place), self.core_land, place)
             return unused
 
@@ -840,7 +862,7 @@
 
 
 def both_kernel(
-    count, sections, cores, depth,
+    names, count, sections, cores, depth,
     rows_hbm, up_hbm, lead_ref, numer_ref, denom_ref, power_ref, attend_gain, attend_bias, attend_mix, fading_ref, bonus_ref,
     feed_gain, feed_bias, feed_mix, entry_hbm, exit_hbm, key_hbm, content_hbm, gate_hbm,
     out_hbm, back_hbm, table_ref, entry_sum, exit_sum, key_sum, content_sum, gate_sum,
@@ -861,9 +883,15 @@
     chunks = length // CHUNK
     passes = 2 * depth
     period = max(2 * count - 2, chunks + 1)
-    peers = Peers(count, width)
+    here = Here(names)
+    peers = Peers(here, count, width, 2 * passes)
     mine = peers.columns(peers.me)
-    micro, core = lax.axis_index("section"), lax.axis_index("seq")
+    micro, core = here.at["section"], here.at["seq"]
+    y, x = lax.div(micro, 2), lax.rem(micro, 2)
+    neighbours = (
+        here.device(seq=1 - core), here.device(section=micro + 1 - 2 * x), here.device(section=micro + 2 - 4 * y)
+    )
+    around = (core, y, x), neighbours
     first = from_tokens(rows_hbm, micro, tokens_ref, token_sems)
     second = from_tokens(up_hbm, micro, back_ref, back_sems)
     for copy in first + second:
@@ -888,8 +916,8 @@
     gather = Gather(peers, pay, (gs, gr))
     tiles = Tiles(peers, stat, (ts, tr))
     scatter = Scatter(peers, part, stage, land, (ss, sr))
-    start_out, wait_out = to_sections(sections, rows_ref, tokens_ref, out_hbm, (os, orr))
-    start_back, wait_back = to_sections(sections, grad_ref, back_ref, back_hbm, (bs, br))
+    start_out, wait_out = to_sections(here, sections, rows_ref, tokens_ref, out_hbm, (os, orr))
+    start_back, wait_back = to_sections(here, sections, grad_ref, back_ref, back_hbm, (bs, br))
 
     def full_copy(k, owner):
         block = full_ref.at[:, :, peers.columns(owner)]
@@ -908,7 +936,7 @@
             grad, core_land, cross_land, own_land, result = parts[place]
             out.append(
                 Summed(
-                    grad, core_land, cross_land, own_land, result.at[level],
+                    around, grad, core_land, cross_land, own_land, result.at[level],
                     (ws.at[level, place], wr.at[level, place]),
                 )
             )
@@ -925,11 +953,11 @@
         other = table_place(k)
         return pltpu.make_async_remote_copy(
             src_ref=small_ref, dst_ref=table_ref.at[owner], send_sem=table_send.at[k - 1], recv_sem=table_recv.at[k - 1],
-            device_id={"section": lax.div(other, cores), "seq": lax.rem(other, cores)}, device_id_type=MESH,
+            device_id=here.device(section=lax.div(other, cores), seq=lax.rem(other, cores)), device_id_type=MESH,
         )
 
     others = [table_place(k) for k in range(1, sections * cores)]
-    peers.greet([{"section": lax.div(other, cores), "seq": lax.rem(other, cores)} for other in others])
+    peers.greet([here.device(section=lax.div(other, cores), seq=lax.rem(other, cores)) for other in others])
     for k in range(1, count):
         full_copy(k, peers.me).start()
     for copy in first:
@@ -944,13 +972,13 @@
             value = scatter.total(c, j - 1)
             tiles.sent(c)
 
-            @pl.when(lax.rem(j, 2) == 1)
+            @pl.when(odd(j, passes) == 1)
             def _():
                 rows_ref[rows, :] += value
 
-            @pl.when(lax.rem(j, 2) == 0)
+            @pl.when(odd(j, passes) == 0)
             def _():
-                level = lax.div(j, 2) - 1
+                level = halves(j, passes) - 1
                 kv_ref[level, rows, :] = value
                 rows_ref[rows, :] += gate_ref[level, rows, :] * value
 
@@ -960,7 +988,7 @@
             middle = jnp.mean(lines, axis=1, keepdims=True)
             center = lines - middle
             square = jnp.sum(center * center, axis=1, keepdims=True)
-            pay[lax.rem(j, 2), rows, mine] = center.astype(jnp.bfloat16)
+            pay[odd(j, passes), rows, mine] = center.astype(jnp.bfloat16)
             tiles.stat[peers.me, c] = to_row_tile(middle, square)
             tiles.start(c)
             gather.start(c, j)
@@ -1018,18 +1046,18 @@
 
         def mix(count_mixed):
             mix_chunk(
-                peers, c, pay.at[lax.rem(j, 2)], tiles, full_ref.at[j], mixed_ref.at[pl.ds(0, count_mixed), pl.ds(0, CHUNK)],
+                peers, c, pay.at[odd(j, passes)], tiles, full_ref.at[j], mixed_ref.at[pl.ds(0, count_mixed), pl.ds(0, CHUNK)],
                 normal_ref.at[j], edge_ref.at[j], std_ref.at[j], last_ref,
             )
 
-        level = lax.div(j, 2)
-
-        @pl.when(lax.rem(j, 2) == 0)
+        level = halves(j, passes)
+
+        @pl.when(odd(j, passes) == 0)
         def _():
             mix(3)
             attend_forward(level, c)
 
-        @pl.when(lax.rem(j, 2) == 1)
+        @pl.when(odd(j, passes) == 1)
         def _():
             mix(2)
             feed_forward(level, c)
@@ -1080,13 +1108,13 @@
             gather.sent(c, passes + which - 1)
             tiles.sent(c)
 
-        @pl.when((which < passes) & (lax.rem(which, 2) == 0))
-        def _():
-            pay[lax.rem(which, 2), rows, mine] = (grad_ref[rows, :] * gate_ref[lax.div(j, 2), rows, :]).astype(jnp.bfloat16)
-
-        @pl.when((which < passes) & (lax.rem(which, 2) == 1))
-        def _():
-            pay[lax.rem(which, 2), rows, mine] = grad_ref[rows, :].astype(jnp.bfloat16)
+        @pl.when((which < passes) & (odd(which, passes) == 0))
+        def _():
+            pay[odd(which, passes), rows, mine] = (grad_ref[rows, :] * gate_ref[halves(j, passes), rows, :]).astype(jnp.bfloat16)
+
+        @pl.when((which < passes) & (odd(which, passes) == 1))
+        def _():
+            pay[odd(which, passes), rows, mine] = grad_ref[rows, :].astype(jnp.bfloat16)
 
         @pl.when(which < passes)
         def _():
@@ -1097,7 +1125,7 @@
             start_back(c)
 
     def attend_backward(j, c):
-        level = lax.div(j, 2)
+        level = halves(j, passes)
         rows = rows_of(c)
         decay = jnp.broadcast_to(jnp.exp(fading_ref[pl.ds(level, 1), :]), (SUB, width))
         bonus = jnp.broadcast_to(bonus_ref[pl.ds(level, 1), :], (SUB, width))
@@ -1142,7 +1170,7 @@
 
     def feed_backward(j, c):
         rows = rows_of(c)
-        level = lax.div(j, 2)
+        level = halves(j, passes)
         gate = gate_ref[level, rows, :]
         pre_grads[0, rows, :] = (grad_ref[rows, :] * gate * kv_ref[level, rows, :] * (1.0 - gate)).astype(jnp.bfloat16)
         for start in range(0, hidden_width, width):
@@ -1167,11 +1195,11 @@
         def _():
             later_ref[...] = jnp.zeros_like(later_ref)
 
-        @pl.when(lax.rem(which, 2) == 0)
+        @pl.when(odd(which, passes) == 0)
         def _():
             feed_backward(j, c)
 
-        @pl.when(lax.rem(which, 2) == 1)
+        @pl.when(odd(which, passes) == 1)
         def _():
             attend_backward(j, c)
 
@@ -1211,9 +1239,11 @@
 
     def when_taken(group, number, t):
         kind, places, later = GROUPS[group]
-        since = t - (base + period * kind + later[number])
-        taken = (since >= 0) & (lax.rem(since, 2 * period) == 0) & (since < 2 * period * depth)
-        return taken, depth - 1 - lax.div(since, 2 * period)
+        taken, chosen = False, 0
+        for level in range(depth):
+            now = t == base + period * kind + later[number] + 2 * period * (depth - 1 - level)
+            taken, chosen = taken | now, chosen + jnp.where(now, level, 0)
+        return taken, chosen
 
     def extra(t):
         for group in range(len(GROUPS)):
@@ -1236,10 +1266,16 @@
     backward_tick = ticks_of(peers, chunks, passes, passes, True, begin_backward, gather, backward, scatter)
     turn = (passes - 1) * period + chunks + count - 1
 
-    def tick(t, unused):
+    def onward(w, i):
+        ends = i == period - 1
+        return jnp.where(ends, w + 1, w), jnp.where(ends, 0, i + 1)
+
+    def tick(t, places):
+        ahead, behind = places
+
         @pl.when(t < passes * period + chunks)
         def _():
-            forward_tick(t)
+            forward_tick(*ahead)
 
         @pl.when(t == turn - 1)
         def _():
@@ -1251,12 +1287,14 @@
 
         @pl.when(t >= turn)
         def _():
-            backward_tick(t - turn)
+            backward_tick(*behind)
             extra(t - turn)
 
-        return unused
-
-    lax.fori_loop(0, turn + final + 1, tick, 0)
+        moved = onward(*behind)
+        return onward(*ahead), tuple(jnp.where(t >= turn, a, b) for a, b in zip(moved, behind))
+
+    start = (jnp.int32(0), jnp.int32(0))
+    lax.fori_loop(0, turn + final + 1, tick, (start, start))
 
     for k in range(1, sections * cores):
         table_copy(k, micro * cores + core).start()
@@ -1321,7 +1359,7 @@
 
 
 def run_fast(
-    residual_entering, upstream_sensitivity, piece_lead_lines, dividend_start, divisor_start, power_offset_start,
+    names, residual_entering, upstream_sensitivity, piece_lead_lines, dividend_start, divisor_start, power_offset_start,
     attend_standard_scale, attend_standard_offset, attend_lag_fractions, fading_log_rate, reward_first_word,
     attend_entry_matrix, attend_exit_matrix, feed_standard_scale, feed_standard_offset, feed_lag_fractions,
     feed_lookup_matrix, feed_content_matrix, feed_gate_matrix,
@@ -1381,7 +1419,7 @@
     ]
     operands += [(value, False) for value in weights]
     out_share, back_share, table, *sums = run_kernel(
-        partial(both_kernel, count, sections, cores, depth), 0, outs, scratch, operands, 3 * flops
+        partial(both_kernel, names, count, sections, cores, depth), 0, outs, scratch, operands, 3 * flops
     )
     return finish(cores, depth, out_share, back_share, table, sums, [weight.shape for weight in weights])
 
@@ -1559,7 +1597,7 @@
     return out_share, back_share, tables, sums
 
 
-def per_device(*arrays):
+def per_device(names, *arrays):
     residual_entering, lookup = arrays[0], arrays[16]
     sections, cores = lax.axis_size("section"), lax.axis_size("seq")
     micros, unused, length, share = residual_entering.shape
@@ -1568,7 +1606,7 @@
     fits = fits and share % 256 == 0 and features % 256 == 0 and hidden % 256 == 0 and hidden % share == 0
     fits = fits and 2 < lax.axis_size("tp") <= LANES // SUB
     if fits:
-        return run_fast(*arrays)
+        return run_fast(names, *arrays)
     out_share, back_share, table, sums = run_plain(*arrays)
     tables = table.reshape(sections, cores, *table.shape[1:])
     mine = lax.dynamic_index_in_dim(tables, lax.axis_index("seq"), 1, keepdims=False)
@@ -1606,7 +1644,7 @@
     state = P(None, None, "seq", "tp")
     tokens = P(None, "seq", "section", "tp")
     return jax.shard_map(
-        per_device,
+        partial(per_device, mesh.axis_names),
         mesh=mesh,
         in_specs=(
             rows, rows, state, state, state, state,

time: 319 us -> 319 us (level)
  no operation moved by 1% of the time
where the time goes in v3:
time: 319 us; the launch traced here: 318 us
  Pallas kernels  317 us (99%)
    pallas_call x1, Pallas kernels, run_kernel(): pl.pallas_call(body, out_shape=[out for out, inside in outs], in_specs=[s...  302 us
    pallas_call x1, Pallas kernels, finish(): pl.pallas_call(partial(finish_kernel, cores, depth), grid=(steps,), out_s...  15.2 us

profile of v3, /device:TPU:9, one launch (start us, length us, event | category | flops | bytes accessed | tf_op | source)
XLA Modules:
  0.0 318.2 jit_solution(6826668201340537850)
XLA Ops:
  0.7 302.2 %shard_map.330 = (f32[4,1,128,256]{3,2,1,0:T(8,128)}, f32[4,1,128,256]{3,2,1,0:T(8,128)}, f32[8,6,8,256]{3,2,1,0:T(8,128)}, bf16[2,3,2,2,2,2,64,256]{7,6,5,4,3,2...) custom-call(f32[4,1,512,256]{3,2,1,0:T(8,128)} %rows_hbm.1, ...), custom_call_target="tpu_custom_call" | custom-call | flops 20937965568 | bytes 33554432 | tf_op jit(solution)/shard_map/pallas_call | solution.py:1344
  302.9 15.2 %shard_map.331 = (f32[512,256]{1,0:T(8,128)}, f32[512,256]{1,0:T(8,128)}, f32[6144,256]{1,0:T(8,128)}, f32[512,1024]{1,0:T(8,128)}, f32[2048,1024]{1,0:T(8,128)}...) custom-call(f32[8,6,8,256]{3,2,1,0:T(8,128)} %get-tuple-element.46.t, ...), custom_call_target="tpu_custom_call" | custom-call | tf_op jit(solution)/shard_map/pallas_call | solution.py:1474

commit v4 on v3

--- a/solution.py
+++ b/solution.py
@@ -857,7 +857,7 @@
 GROUPS = (
     (0, (1,), (1, 2, 4, 5, 6, 11)),
     (0, (0, 2), (0, 1, 3, 4, 5, 11)),
-    (1, (3, 4), (1, 2, 4, 5, 6, 12)),
+    (1, (4, 3), (1, 2, 4, 5, 6, 12)),
 )
 
 
@@ -956,14 +956,13 @@
             device_id=here.device(section=lax.div(other, cores), seq=lax.rem(other, cores)), device_id_type=MESH,
         )
 
+    for copy in first:
+        copy.wait()
+    to_stretches(tokens_ref, rows_ref)
     others = [table_place(k) for k in range(1, sections * cores)]
     peers.greet([here.device(section=lax.div(other, cores), seq=lax.rem(other, cores)) for other in others])
     for k in range(1, count):
         full_copy(k, peers.me).start()
-    for copy in first:
-        copy.wait()
-    to_stretches(tokens_ref, rows_ref)
-
     def begin_forward(j, c):
         rows = rows_of(c)
 
@@ -1264,7 +1263,7 @@
 
     forward_tick = ticks_of(peers, chunks, passes, 0, False, begin_forward, gather, forward, scatter)
     backward_tick = ticks_of(peers, chunks, passes, passes, True, begin_backward, gather, backward, scatter)
-    turn = (passes - 1) * period + chunks + count - 1
+    turn = (passes - 1) * period + chunks + count - 2
 
     def onward(w, i):
         ends = i == period - 1

time: 319 us -> 320 us (level)
  no operation moved by 1% of the time
where the time goes in v4:
time: 320 us
  Pallas kernels  319 us (100%)
    pallas_call x1, Pallas kernels, run_kernel(): pl.pallas_call(body, out_shape=[out for out, inside in outs], in_specs=[s...  304 us
    pallas_call x1, Pallas kernels, finish(): pl.pallas_call(partial(finish_kernel, cores, depth), grid=(steps,), out_s...  15.2 us

profile of v4, /device:TPU:9, one launch (start us, length us, event | category | flops | bytes accessed | tf_op | source)
XLA Modules:
  0.0 320.1 jit_solution(5101368502468366658)
XLA Ops:
  0.7 304.1 %shard_map.330 = (f32[4,1,128,256]{3,2,1,0:T(8,128)}, f32[4,1,128,256]{3,2,1,0:T(8,128)}, f32[8,6,8,256]{3,2,1,0:T(8,128)}, bf16[2,3,2,2,2,2,64,256]{7,6,5,4,3,2...) custom-call(f32[4,1,512,256]{3,2,1,0:T(8,128)} %rows_hbm.1, ...), custom_call_target="tpu_custom_call" | custom-call | flops 20937965568 | bytes 33554432 | tf_op jit(solution)/shard_map/pallas_call | solution.py:1343
  304.8 15.2 %shard_map.331 = (f32[512,256]{1,0:T(8,128)}, f32[512,256]{1,0:T(8,128)}, f32[6144,256]{1,0:T(8,128)}, f32[512,1024]{1,0:T(8,128)}, f32[2048,1024]{1,0:T(8,128)}...) custom-call(f32[8,6,8,256]{3,2,1,0:T(8,128)} %get-tuple-element.46.t, ...), custom_call_target="tpu_custom_call" | custom-call | tf_op jit(solution)/shard_map/pallas_call | solution.py:1473

commit v5 on v3

--- a/solution.py
+++ b/solution.py
@@ -855,9 +855,9 @@
 
 
 GROUPS = (
-    (0, (1,), (1, 2, 4, 5, 6, 11)),
-    (0, (0, 2), (0, 1, 3, 4, 5, 11)),
-    (1, (3, 4), (1, 2, 4, 5, 6, 12)),
+    (0, (1,), (1, 3, 5, 7, 9, 12)),
+    (0, (0, 2), (0, 2, 4, 6, 8, 11)),
+    (1, (3, 4), (1, 2, 4, 5, 7, 12)),
 )
 
 

time: 319 us -> 322 us (level); the launches traced: 318 us -> 317 us
  no operation moved by 1% of the time
where the time goes in v5:
time: 322 us; the launch traced here: 317 us
  Pallas kernels  316 us (98%)
    pallas_call x1, Pallas kernels, run_kernel(): pl.pallas_call(body, out_shape=[out for out, inside in outs], in_specs=[s...  301 us
    pallas_call x1, Pallas kernels, finish(): pl.pallas_call(partial(finish_kernel, cores, depth), grid=(steps,), out_s...  15.2 us

profile of v5, /device:TPU:9, one launch (start us, length us, event | category | flops | bytes accessed | tf_op | source)
XLA Modules:
  0.0 317.0 jit_solution(147937828478154968)
XLA Ops:
  0.7 301.0 %shard_map.330 = (f32[4,1,128,256]{3,2,1,0:T(8,128)}, f32[4,1,128,256]{3,2,1,0:T(8,128)}, f32[8,6,8,256]{3,2,1,0:T(8,128)}, bf16[2,3,2,2,2,2,64,256]{7,6,5,4,3,2...) custom-call(f32[4,1,512,256]{3,2,1,0:T(8,128)} %rows_hbm.1, ...), custom_call_target="tpu_custom_call" | custom-call | flops 20937965568 | bytes 33554432 | tf_op jit(solution)/shard_map/pallas_call | solution.py:1344
  301.7 15.2 %shard_map.331 = (f32[512,256]{1,0:T(8,128)}, f32[512,256]{1,0:T(8,128)}, f32[6144,256]{1,0:T(8,128)}, f32[512,1024]{1,0:T(8,128)}, f32[2048,1024]{1,0:T(8,128)}...) custom-call(f32[8,6,8,256]{3,2,1,0:T(8,128)} %get-tuple-element.46.t, ...), custom_call_target="tpu_custom_call" | custom-call | tf_op jit(solution)/shard_map/pallas_call | solution.py:1474

commit v6 on v3

--- a/solution.py
+++ b/solution.py
@@ -894,25 +894,9 @@
     around = (core, y, x), neighbours
     first = from_tokens(rows_hbm, micro, tokens_ref, token_sems)
     second = from_tokens(up_hbm, micro, back_ref, back_sems)
-    for copy in first + second:
+    for copy in first:
         copy.start()
-    weights = load(
-        (
-            (entry_hbm, entry_ref), (exit_hbm, exit_ref), (key_hbm, w_key), (content_hbm, w_content),
-            (gate_hbm, w_gate),
-        ),
-        load_sems,
-        0,
-    )
     full_ref[...] = jnp.zeros_like(full_ref)
-    for j in range(2 * depth):
-        level = j // 2
-        gain, bias, mix = (attend_gain, attend_bias, attend_mix) if j % 2 == 0 else (feed_gain, feed_bias, feed_mix)
-        full_ref[j, 0:1, mine] = gain[level : level + 1, :]
-        full_ref[j, 1:2, mine] = bias[level : level + 1, :]
-        full_ref[j, 2:3, mine] = lead_ref[j, micro]
-        for i in range(mix.shape[0] if j % 2 == 0 else mix.shape[1]):
-            full_ref[j, 3 + i : 4 + i, mine] = mix[i, level : level + 1] if j % 2 == 0 else mix[level, i : i + 1]
     gather = Gather(peers, pay, (gs, gr))
     tiles = Tiles(peers, stat, (ts, tr))
     scatter = Scatter(peers, part, stage, land, (ss, sr))
@@ -958,10 +942,28 @@
 
     others = [table_place(k) for k in range(1, sections * cores)]
     peers.greet([here.device(section=lax.div(other, cores), seq=lax.rem(other, cores)) for other in others])
+    for j in range(2 * depth):
+        level = j // 2
+        gain, bias, mix = (attend_gain, attend_bias, attend_mix) if j % 2 == 0 else (feed_gain, feed_bias, feed_mix)
+        full_ref[j, 0:1, mine] = gain[level : level + 1, :]
+        full_ref[j, 1:2, mine] = bias[level : level + 1, :]
+        full_ref[j, 2:3, mine] = lead_ref[j, micro]
+        for i in range(mix.shape[0] if j % 2 == 0 else mix.shape[1]):
+            full_ref[j, 3 + i : 4 + i, mine] = mix[i, level : level + 1] if j % 2 == 0 else mix[level, i : i + 1]
     for k in range(1, count):
         full_copy(k, peers.me).start()
     for copy in first:
         copy.wait()
+    weights = load(
+        (
+            (entry_hbm, entry_ref), (exit_hbm, exit_ref), (key_hbm, w_key), (content_hbm, w_content),
+            (gate_hbm, w_gate),
+        ),
+        load_sems,
+        0,
+    )
+    for copy in second:
+        copy.start()
     to_stretches(tokens_ref, rows_ref)
 
     def begin_forward(j, c):
@@ -1264,7 +1266,7 @@
 
     forward_tick = ticks_of(peers, chunks, passes, 0, False, begin_forward, gather, forward, scatter)
     backward_tick = ticks_of(peers, chunks, passes, passes, True, begin_backward, gather, backward, scatter)
-    turn = (passes - 1) * period + chunks + count - 1
+    turn = (passes - 1) * period + chunks + count - 2
 
     def onward(w, i):
         ends = i == period - 1

time: 319 us -> 316 us (level)
  no operation moved by 1% of the time
where the time goes in v6:
time: 316 us
  Pallas kernels  315 us (100%)
    pallas_call x1, Pallas kernels, run_kernel(): pl.pallas_call(body, out_shape=[out for out, inside in outs], in_specs=[s...  300 us
    pallas_call x1, Pallas kernels, finish(): pl.pallas_call(partial(finish_kernel, cores, depth), grid=(steps,), out_s...  15.2 us

profile of v6, /device:TPU:9, one launch (start us, length us, event | category | flops | bytes accessed | tf_op | source)
XLA Modules:
  0.0 315.6 jit_solution(6548746968285564950)
XLA Ops:
  0.7 299.6 %shard_map.330 = (f32[4,1,128,256]{3,2,1,0:T(8,128)}, f32[4,1,128,256]{3,2,1,0:T(8,128)}, f32[8,6,8,256]{3,2,1,0:T(8,128)}, bf16[2,3,2,2,2,2,64,256]{7,6,5,4,3,2...) custom-call(f32[4,1,512,256]{3,2,1,0:T(8,128)} %rows_hbm.1, ...), custom_call_target="tpu_custom_call" | custom-call | flops 20937965568 | bytes 33554432 | tf_op jit(solution)/shard_map/pallas_call | solution.py:1346
  300.3 15.2 %shard_map.331 = (f32[512,256]{1,0:T(8,128)}, f32[512,256]{1,0:T(8,128)}, f32[6144,256]{1,0:T(8,128)}, f32[512,1024]{1,0:T(8,128)}, f32[2048,1024]{1,0:T(8,128)}...) custom-call(f32[8,6,8,256]{3,2,1,0:T(8,128)} %get-tuple-element.46.t, ...), custom_call_target="tpu_custom_call" | custom-call | tf_op jit(solution)/shard_map/pallas_call | solution.py:1476

commit v7 on v6

--- a/solution.py
+++ b/solution.py
@@ -855,8 +855,8 @@
 
 
 GROUPS = (
-    (0, (1,), (1, 2, 4, 5, 6, 11)),
-    (0, (0, 2), (0, 1, 3, 4, 5, 11)),
+    (0, (1, 2), (1, 2, 4, 5, 6, 11)),
+    (0, (0,), (0, 1, 3, 4, 5, 11)),
     (1, (3, 4), (1, 2, 4, 5, 6, 12)),
 )
 

time: 316 us -> 317 us (level)
  no operation moved by 1% of the time
where the time goes in v7:
time: 317 us; the launch traced here: 315 us
  Pallas kernels  314 us (99%)
    pallas_call x1, Pallas kernels, run_kernel(): pl.pallas_call(body, out_shape=[out for out, inside in outs], in_specs=[s...  299 us
    pallas_call x1, Pallas kernels, finish(): pl.pallas_call(partial(finish_kernel, cores, depth), grid=(steps,), out_s...  15.2 us

profile of v7, /device:TPU:9, one launch (start us, length us, event | category | flops | bytes accessed | tf_op | source)
XLA Modules:
  0.0 315.2 jit_solution(7695280722895535259)
XLA Ops:
  0.7 299.2 %shard_map.330 = (f32[4,1,128,256]{3,2,1,0:T(8,128)}, f32[4,1,128,256]{3,2,1,0:T(8,128)}, f32[8,6,8,256]{3,2,1,0:T(8,128)}, bf16[2,3,2,2,2,2,64,256]{7,6,5,4,3,2...) custom-call(f32[4,1,512,256]{3,2,1,0:T(8,128)} %rows_hbm.1, ...), custom_call_target="tpu_custom_call" | custom-call | flops 20937965568 | bytes 33554432 | tf_op jit(solution)/shard_map/pallas_call | solution.py:1346
  299.9 15.2 %shard_map.331 = (f32[512,256]{1,0:T(8,128)}, f32[512,256]{1,0:T(8,128)}, f32[6144,256]{1,0:T(8,128)}, f32[512,1024]{1,0:T(8,128)}, f32[2048,1024]{1,0:T(8,128)}...) custom-call(f32[8,6,8,256]{3,2,1,0:T(8,128)} %get-tuple-element.46.t, ...), custom_call_target="tpu_custom_call" | custom-call | tf_op jit(solution)/shard_map/pallas_call | solution.py:1476
